TPU v7x, 256 devices: a whole 4x4x8 slice. The times are simulated.
256 devices in a mesh: tm: 64 (over y, z, core), space: 4 (over x).
Axes of the slice: x: 4, y: 4, z: 8, core: 2. Of those that a mesh axis runs over, the one named last changes fastest.
Arguments:
- frames: bfloat16 [256, 32, 24, 384], P('tm', 'space'), may hold values from -6 to 6
- conv_weight: bfloat16 [27, 384, 384], replicated, may hold values from -0.0625 to 0.0625
- head_weight: bfloat16 [384, 32], replicated, may hold values from -0.3125 to 0.3125
- clip_len: int32 [21], replicated, may hold values from 1 to 21, 256 in all
Outputs:
- latent: float32 [256, 32, 24, 32], P('tm', 'space')
- loss: float32 [], replicated
- weight_grad: float32 [27, 384, 384], P(None, 'tm', 'space')
- head_grad: float32 [384, 32], P('tm', 'space')
Inputs may be any that keep to these rules, and one draw needn't show every extreme that they name: `clip_len`: the lengths sum to 256; the longest clip has exactly 21 frames.
All inputs are finite; a program needn't handle non-finite values.
Results may differ from a plain program's by a relative error of at most 0.003.
Values may be sent and summed in bfloat16 or wider, within the bound.
No kernel may reach another device: no remote copies, remote signals or barrier semaphores. Data moves between devices by JAX's collectives and lax.ppermute only.
A program may use at most 256 MiB of HBM per device.

v0:
```python
import functools

import jax
import jax.numpy as jnp
import numpy as np
from jax import lax
from jax.experimental import pallas as pl
from jax.experimental.pallas import tpu as pltpu
from jax.sharding import PartitionSpec as P

F32 = jnp.float32
B16 = jnp.bfloat16
COLS = 24
LIMIT = 56 * 1024 * 1024
NT = (((1,), (1,)), ((), ()))
TN = (((0,), (0,)), ((), ()))


def dot(a, b, dims=None):
    if dims is None:
        return jnp.dot(a, b, preferred_element_type=F32)
    return lax.dot_general(a, b, dims, preferred_element_type=F32)


def call(kernel, outs, scratch=(), **kw):
    params = pltpu.CompilerParams(vmem_limit_bytes=LIMIT)
    return pl.pallas_call(kernel, out_shape=outs, scratch_shapes=list(scratch), compiler_params=params, **kw)


def smem():
    return pl.BlockSpec(memory_space=pltpu.SMEM)


def vmem():
    return pl.BlockSpec(memory_space=pltpu.VMEM)


def place(nz):
    t = lax.axis_index("tm")
    k = lax.div(t, 2)
    return lax.rem(t, 2), lax.axis_index("space"), lax.div(k, nz), lax.rem(k, nz), k


def half_table(chans, run, ny, nz):
    lane = np.arange(chans // 2)
    block = wide(run) * nz
    spot = (lane // run // nz) * block + (lane % run) * nz + lane // run % nz
    table = np.zeros((2, chans, ny * block), np.float32)
    for core in range(2):
        table[core, (lane // run) * 2 * run + core * run + lane % run, spot] = 1
    return table


def wide(run):
    return -(-run // 8) * 8


def first_kernel(x_ref, top_ref, bot_ref):
    nf, band, chans = x_ref.shape
    for f in range(nf):
        wide_frame = x_ref[f].astype(F32)
        top_ref[f] = wide_frame[:COLS].astype(B16)
        bot_ref[f] = wide_frame[band - COLS :].astype(B16)


def frame_of(top, mid, bot):
    return jnp.concatenate([top.astype(F32), mid.astype(F32), bot.astype(F32)], axis=0)


def ends_kernel(x_ref, top_ref, bot_ref, ends_ref):
    nf = x_ref.shape[0]
    for f in range(2):
        g = nf - 2 + f
        ends_ref[f] = frame_of(top_ref[g], x_ref[g], bot_ref[g]).astype(B16)


def choose_kernel(f0, f1, f2, f3, table_ref, own_ref, oth_ref, wide_ref):
    c, x = lax.rem(lax.axis_index("tm"), 2), lax.axis_index("space")
    band = f0.shape[1]

    for d, ref in enumerate((f0, f1, f2, f3)):
        wide_ref[pl.ds(pl.multiple_of(lax.rem(x - d + 4, 4) * band, band), band)] = ref[0]
    both = dot(wide_ref[...], table_ref[c]).astype(B16)
    lanes = own_ref.shape[2]
    own_ref[0] = both[:, :lanes]
    oth_ref[0] = both[:, lanes:]


def forward_kernel(len_ref, x_ref, ends_ref, top_ref, bot_ref, w_ref, hw_ref,
                   lat_ref, d0, d1, d2, d3, pre_ref, wide_ref, turned_ref, head_ref, held_ref, sem):
    nf, band, chans = x_ref.shape
    rows = band + 2 * COLS
    loads = [pltpu.make_async_copy(w_ref.at[dt], held_ref.at[dt], sem.at[dt]) for dt in range(3)]
    for load in loads:
        load.start()
    col = lax.rem(lax.broadcasted_iota(jnp.int32, (rows, 1), 0), COLS)
    for f in range(nf + 2):
        if f < 2:
            v = ends_ref[f].astype(F32)
        else:
            v = frame_of(top_ref[f - 2], x_ref[f - 2], bot_ref[f - 2])
        for dw in range(3):
            if dw == 0:
                s = jnp.where(col > 0, pltpu.roll(v, 1, 0), 0.0)
            elif dw == 2:
                s = jnp.where(col < COLS - 1, pltpu.roll(v, rows - 1, 0), 0.0)
            else:
                s = v
            for dh in range(3):
                q = dh * 3 + dw
                wide_ref[f * band : (f + 1) * band, q * chans : (q + 1) * chans] = s[
                    dh * COLS : dh * COLS + band
                ].astype(B16)

    t, xs = lax.axis_index("tm"), lax.axis_index("space")
    pos = [jnp.int32(0)] * nf
    start = jnp.int32(0)
    for j in range(len_ref.shape[0]):
        for f in range(nf):
            pos[f] = jnp.where(t * nf + f >= start, t * nf + f - start, pos[f])
        start = start + len_ref[j]
    for dt in range(3):
        loads[dt].wait()
        part = dot(wide_ref[dt * band : (dt + nf) * band, :], held_ref[dt])
        for f in range(nf):
            keep = jnp.where(pos[f] >= 2 - dt, 1.0, 0.0)
            piece = keep * part[f * band : (f + 1) * band]
            if dt == 0:
                pre_ref[f * band : (f + 1) * band] = piece
            else:
                pre_ref[f * band : (f + 1) * band] += piece

    zdim = lat_ref.shape[1] // 2
    row = lax.broadcasted_iota(jnp.int32, (16, 128), 0)
    kf = jnp.zeros((16, 128), F32)
    for f in range(nf):
        at = slice(f * band, (f + 1) * band)
        pre = pre_ref[at]
        sig = 1.0 / (1.0 + jnp.exp(-pre))
        act = (pre * sig).astype(B16)
        lat = dot(act, hw_ref[...], NT)
        lat_ref[at] = lat
        lane = lax.broadcasted_iota(jnp.int32, lat.shape, 1)
        grow = jnp.exp(lat) - 1.0
        term = jnp.where(lane < zdim, lat * lat, grow - lat)
        kf = jnp.where(lax.rem(row, nf) == f, 0.5 * jnp.sum(term), kf)
        dlat = jnp.where(lane < zdim, lat, 0.5 * grow).astype(B16)
        dact = dot(dlat, hw_ref[...])
        pre_ref[at] = (dact * sig * (1.0 + pre * (1.0 - sig))).astype(B16).astype(F32)
        head_ref[f] = dot(dlat, act, TN)
    high = kf.astype(B16).astype(F32)
    mid = (kf - high).astype(B16).astype(F32)
    kf = jnp.where(row < nf, high, jnp.where(row < 2 * nf, mid, jnp.where(row < 3 * nf, kf - high - mid, 0.0)))
    turned_ref[...] = jnp.transpose(pre_ref[...], (1, 0)).astype(B16)
    block = chans // 4
    hblock = 2 * zdim // 4
    for d, ref in enumerate((d0, d1, d2, d3)):
        to = lax.rem(xs + d, 4)
        ref[:16, :128] = kf.astype(B16)
        ref[:16, 128:] = jnp.zeros((16, ref.shape[1] - 128), B16)
        ref[32:] = turned_ref[pl.ds(pl.multiple_of(to * block, block), block), :]
        heads = [head_ref[f, pl.ds(pl.multiple_of(to * hblock, hblock), hblock), :] for f in range(nf)]
        pad = ref.shape[1] - 2 * chans
        if pad:
            heads = [jnp.concatenate([h, jnp.zeros((hblock, pad // 2), F32)], axis=1) for h in heads]
        both = jnp.concatenate(
            [jnp.concatenate(heads[:2], axis=1), jnp.concatenate(heads[2:], axis=1)], axis=0
        )
        ref[16:32] = both.astype(B16)


def clip_kernel(*refs):
    c, x = lax.rem(lax.axis_index("tm"), 2), lax.axis_index("space")
    given, (sums_ref, tail_ref) = (refs[:4], refs[4:8]), refs[8:]
    sums = []
    for four in given:
        v = four[0][:16, :128].astype(F32)
        for ref in four[1:]:
            v = v + ref[:16, :128].astype(F32)
        sums.append(v[:4] + v[4:8] + v[8:12])
    for core in range(2):

        @pl.when(c == core)
        def _():
            sums_ref[...] = jnp.concatenate([sums[core], sums[1 - core]], axis=0)
            for d in range(4):
                tail_ref[lax.rem(x - d + 4, 4)] = given[core][d][32:, :]


def weight_kernel(ny, nz, per_frame, len_ref, left_ref, mid_ref, right_ref, next_ref, a0, a1, a2, a3, b0, b1, b2, b3,
                  x_ref, xo_ref, table_ref, *refs):
    sends, (held_ref, taps_ref, acc_ref, out_ref, xs_ref, g_ref, keep_ref, sem) = refs[:ny], refs[ny:]
    c, x, y, _, k = place(nz)
    copies = []
    for core, given, s in ((c, (a0, a1, a2, a3), 0), (1 - c, (b0, b1, b2, b3), 1)):
        for d, ref in enumerate(given):
            copies.append(pltpu.make_async_copy(ref, held_ref.at[core, lax.rem(x - d + 4, 4)], sem.at[s, d]))
    for core, ref, s in ((c, x_ref, 0), (1 - c, xo_ref, 1)):
        copies.append(pltpu.make_async_copy(ref, xs_ref.at[pl.ds(4 * core, 4)], sem.at[2, s]))
    for copy in copies:
        copy.start()
    full = x_ref.shape[1]
    band = full // 4
    block = taps_ref.shape[1] // 9
    chans = table_ref.shape[1]
    lanes = acc_ref.shape[2]
    hblock = 8
    half = full // 2
    window = jnp.concatenate(
        [left_ref[0], left_ref[1], left_ref[2], mid_ref[...], right_ref[0], right_ref[1], right_ref[2]], axis=0
    )
    chip = mid_ref.shape[0]
    wids = chip * (k - 3) + lax.broadcasted_iota(jnp.int32, window.shape, 0)
    ids = chip * k + lax.broadcasted_iota(jnp.int32, g_ref.shape, 0)
    total = jnp.zeros(g_ref.shape, F32)
    lens = jnp.ones(g_ref.shape, F32)
    pos = jnp.full(g_ref.shape, -1, jnp.int32)
    start = jnp.int32(0)
    for j in range(len_ref.shape[0]):
        size = len_ref[j]
        inside = jnp.where((wids >= start) & (wids < start + size), window, 0.0)
        mine = (ids >= start) & (ids < start + size)
        total = jnp.where(mine, jnp.sum(inside, axis=0, keepdims=True), total)
        lens = jnp.where(mine, size.astype(F32), lens)
        pos = jnp.where(mine, ids - start, pos)
        start = start + size
    gain = lens / (lens * per_frame + total)
    g_ref[...] = gain
    for dt in range(3):
        keep_ref[dt] = jnp.where(pos >= 2 - dt, gain, 0.0)
    row = lax.broadcasted_iota(jnp.int32, g_ref.shape, 0)
    loss = jnp.where((pos == 0) & (row < chip), lens * jnp.log1p(total / (lens * per_frame)), 0.0)
    loss = jnp.sum(loss, axis=0, keepdims=True)
    hsum = jnp.zeros((hblock, chans), F32)
    for copy in copies[:8]:
        copy.wait()
    for core in range(2):
        for xs in range(4):
            tail = held_ref[core, xs, 16:32, :].astype(F32)
            for f in range(4):
                part = tail[(f // 2) * hblock : (f // 2 + 1) * hblock, (f % 2) * half : (f % 2) * half + chans]
                hsum = hsum + g_ref[core * 4 + f : core * 4 + f + 1, :1] * part
    acc_ref[...] = jnp.zeros(acc_ref.shape, F32)
    lane = lax.broadcasted_iota(jnp.int32, (1, full), 1)
    col = lax.rem(lane, COLS)
    line = lane // COLS

    def build(f):
        core, lf = f // 4 % 2, f % 4
        frame = jnp.zeros((block, full), F32)
        for xs in range(4):
            if f < 8:
                v = held_ref[core, xs, 32:, :].astype(F32)
            else:
                v = next_ref[xs].astype(F32)
                v = jnp.concatenate([v, jnp.zeros_like(v)], axis=1)
            shift = ((xs - lf) * band) % full
            if shift:
                v = pltpu.roll(v, shift, 1)
            frame = jnp.where(lane // band == xs, v, frame)
        for dw in range(3):
            if dw == 0:
                v = jnp.where(col < COLS - 1, pltpu.roll(frame, full - 1, 1), 0.0)
            elif dw == 2:
                v = jnp.where(col > 0, pltpu.roll(frame, 1, 1), 0.0)
            else:
                v = frame
            for dh in range(3):
                if dh == 0:
                    s = jnp.where(line < full // COLS - 1, pltpu.roll(v, full - COLS, 1), 0.0)
                elif dh == 2:
                    s = jnp.where(line > 0, pltpu.roll(v, COLS, 1), 0.0)
                else:
                    s = v
                q = dh * 3 + dw
                taps_ref[f % 2, q * block : (q + 1) * block, :] = s.astype(B16)

    build(0)
    for copy in copies[8:]:
        copy.wait()
    for f in range(10):
        if f < 9:
            build(f + 1)
        for dt in range(3):
            if 0 <= f - 2 + dt < 8:
                scale = keep_ref[dt, f : f + 1, :1]
                acc_ref[dt, : 9 * block] += scale * dot(taps_ref[f % 2], xs_ref[f - 2 + dt])
    direct = table_ref[c, :, :lanes]
    high = hsum.astype(B16)
    low = (hsum - high.astype(F32)).astype(B16)
    acc_ref[0, 9 * block : 9 * block + hblock] = dot(high, direct) + dot(low, direct)
    loss = jnp.broadcast_to(loss[:, :1], (8, lanes))
    top = loss.astype(B16).astype(F32)
    mid = (loss - top).astype(B16).astype(F32)
    acc_ref[1, 9 * block : 9 * block + 8] = top
    acc_ref[1, 9 * block + 8 : 9 * block + 16] = mid
    acc_ref[1, 9 * block + 16 : 9 * block + 24] = loss - top - mid
    rows = sends[0].shape[1]
    ystep = lanes // ny
    for dt in range(3):
        out_ref[...] = jnp.transpose(acc_ref[dt], (1, 0))
        for d, ref in enumerate(sends):
            to = lax.rem(y + d, ny)
            ref[dt] = out_ref[pl.ds(pl.multiple_of(to * ystep, 8), rows), :].astype(ref.dtype)


def add_kernel(ny, nz, run, *refs):
    gets, (keep_ref, send_ref, sum_ref, part_ref) = refs[:ny], refs[ny:]
    total = gets[0][...]
    for ref in gets[1:]:
        total = total + ref[...].astype(F32)
    chunk = sum_ref.shape[3]
    for i in range(sum_ref.shape[0]):
        sum_ref[i] = total[:, :, i * chunk : (i + 1) * chunk]
    part_ref[...] = jnp.zeros(part_ref.shape, F32)
    step = part_ref.shape[1] // 3
    for z in range(nz):
        for dt in range(3):
            for i in range(sum_ref.shape[0]):
                part_ref[z, dt * step : dt * step + run, i * chunk : (i + 1) * chunk] = sum_ref[
                    i, dt, pl.ds(z, run, stride=nz), :
                ]
    side = lax.rem(place(nz)[3], 2)
    for m in range(nz // 2):
        keep_ref[m] = part_ref[2 * m + side]
        send_ref[m] = part_ref[2 * m + 1 - side].astype(B16)


def pair_kernel(nz, keep_ref, got_ref, *refs):
    sends, sum_ref = refs[:-1], refs[-1]
    sum_ref[...] = keep_ref[...] + got_ref[...].astype(F32)
    m = lax.div(place(nz)[3], 2)
    for d, ref in enumerate(sends):
        ref[...] = sum_ref[lax.rem(m + d, nz // 2)].astype(ref.dtype)


def last_kernel(count, *refs):
    parts, (weight_ref, head_ref, loss_ref) = refs[:count], refs[count:]
    total = parts[0][...]
    for ref in parts[1:]:
        total = total + ref[...].astype(F32)
    run, _, block = weight_ref.shape
    step = total.shape[0] // 3
    for dt in range(3):
        for q in range(9):
            weight_ref[:, dt * 9 + q, :] = total[dt * step : dt * step + run, q * block : (q + 1) * block]
    base = 9 * block
    head_ref[...] = total[:run, base : base + head_ref.shape[1]]
    loss = total[step : step + 1, base : base + 1]
    loss = loss + total[step : step + 1, base + 8 : base + 9]
    loss_ref[...] = loss + total[step : step + 1, base + 16 : base + 17]


def body(frames, conv_weight, head_weight, clip_len):
    nf, nrow, ncol, chans = frames.shape
    band = nrow * ncol
    cells = nf * band
    count = lax.axis_size("tm")
    ny = 4 if count == 64 else 2
    nz = count // 2 // ny
    run = chans // count
    chip = 2 * nf
    shape = jax.ShapeDtypeStruct

    def index(yy, zz, cc):
        return ((yy % ny) * nz + zz % nz) * 2 + cc

    every = [(yy, zz, cc) for yy in range(ny) for zz in range(nz) for cc in range(2)]

    def over_core(v):
        return lax.ppermute(v, "tm", [(i, i ^ 1) for i in range(count)])

    def over_chip(v, d):
        return lax.ppermute(v, "tm", [(i, (i + 2 * d) % count) for i in range(count)])

    def over_x(v, d):
        return lax.ppermute(v, "space", [(i, (i + d) % 4) for i in range(4)])

    def over_y(v, d):
        return lax.ppermute(v, "tm", [(index(a, b, e), index(a + d, b, e)) for a, b, e in every])

    def over_z(v, d):
        return lax.ppermute(v, "tm", [(index(a, b, e), index(a, b + d, e)) for a, b, e in every])

    table = half_table(chans, run, ny, nz)
    lanes = table.shape[2]
    table = np.concatenate([table, table[::-1]], axis=2)
    table = jnp.asarray(table, B16)
    flat = frames.reshape(nf, band, chans)
    edge = shape((nf, ncol, chans), B16)
    top, bot = call(first_kernel, [edge, edge], name="first")(flat)
    top, bot = (
        lax.ppermute(bot, "space", [(i, i + 1) for i in range(3)]),
        lax.ppermute(top, "space", [(i + 1, i) for i in range(3)]),
    )
    flat, top, bot = lax.optimization_barrier((flat, top, bot))
    flats = [flat] + [over_x(flat, d) for d in (1, 2, 3)]
    ends = call(ends_kernel, shape((2, band + 2 * ncol, chans), B16), name="ends")(flat, top, bot)
    ends = lax.ppermute(ends, "tm", [(i, i + 1) for i in range(count - 1)])

    whole = lambda *dims: pl.BlockSpec(dims, lambda i: (0,) * len(dims))
    zlat = head_weight.shape[1]
    hblock = zlat // 4
    block = chans // 4
    message = shape((32 + block, cells), B16)
    latent, *mine_d = call(
        forward_kernel,
        [shape((cells, zlat), F32)] + [message] * 4,
        [
            pltpu.VMEM((cells, chans), F32),
            pltpu.VMEM(((nf + 2) * band, 9 * chans), B16),
            pltpu.VMEM((chans, cells), B16),
            pltpu.VMEM((nf, zlat, chans), F32),
            pltpu.VMEM((3, 9 * chans, chans), B16),
            pltpu.SemaphoreType.DMA((3,)),
        ],
        grid=(1,),
        in_specs=[smem()]
        + [whole(*v.shape) for v in (flat, ends, top, bot)]
        + [pl.BlockSpec(memory_space=pl.ANY), whole(zlat, chans)],
        out_specs=[whole(cells, zlat)] + [whole(*message.shape)] * 4,
        name="forward",
    )(clip_len, flat, ends, top, bot, conv_weight.reshape(3, 9 * chans, chans), head_weight.T)
    mine_d, flats = lax.optimization_barrier((mine_d, flats))
    mine_d = [mine_d[0]] + [over_x(mine_d[d], d) for d in (1, 2, 3)]
    chosen = shape((4, 4 * band, lanes), B16)
    spec = pl.BlockSpec((1, 4 * band, lanes), lambda i: (i, 0, 0))
    xown, xoth = call(
        choose_kernel,
        [chosen, chosen],
        [pltpu.VMEM((4 * band, chans), B16)],
        grid=(4,),
        in_specs=[pl.BlockSpec((1, band, chans), lambda i: (i, 0, 0))] * 4 + [whole(*table.shape)],
        out_specs=[spec, spec],
        name="choose",
    )(*flats, table)
    mine_d, xoth = lax.optimization_barrier((mine_d, xoth))
    core_d = [over_core(v) for v in mine_d]
    xoth = over_core(xoth)

    front = pl.BlockSpec((message.shape[0], 2 * band), lambda i: (0, 0))
    kchip, tail = call(
        clip_kernel,
        [shape((chip, 128), F32), shape((4, block, 2 * band), B16)],
        grid=(1,),
        in_specs=[front] * 8,
        out_specs=[whole(chip, 128), whole(4, block, 2 * band)],
        name="clip",
    )(*mine_d, *core_d)
    tail = over_chip(tail, -1)
    triple = jnp.stack([over_chip(kchip, 1), kchip, over_chip(kchip, -1)])
    left, right = over_chip(triple, 2), over_chip(triple, -2)

    rows = run * nz
    wrow = 9 * block + 32
    sends = call(
        functools.partial(weight_kernel, ny, nz, float(4 * band)),
        [shape((3, rows, wrow), F32)] + [shape((3, rows, wrow), B16)] * (ny - 1),
        [
            pltpu.VMEM((2, 4) + message.shape, B16),
            pltpu.VMEM((2, 9 * block, 4 * band), B16),
            pltpu.VMEM((3, wrow, lanes), F32),
            pltpu.VMEM((lanes, wrow), F32),
            pltpu.VMEM((8, 4 * band, lanes), B16),
            pltpu.VMEM((2 * chip, 128), F32),
            pltpu.VMEM((3, 2 * chip, 128), F32),
            pltpu.SemaphoreType.DMA((3, 4)),
        ],
        in_specs=[smem()] + [vmem()] * 4 + [pl.BlockSpec(memory_space=pl.ANY)] * 10 + [vmem()],
        name="weight",
    )(clip_len, left, kchip, right, tail, *mine_d, *core_d, xown, xoth, table)
    gets = [sends[0]] + [over_y(sends[d], d) for d in range(1, ny)]
    step = wide(run)
    chunk = 128 if wrow % 128 == 0 else wrow
    half = shape((nz // 2, 3 * step, wrow), F32)
    kept, sent = call(
        functools.partial(add_kernel, ny, nz, run),
        [half, shape(half.shape, B16)],
        [pltpu.VMEM((wrow // chunk, 3, rows, chunk), F32), pltpu.VMEM((nz, 3 * step, wrow), F32)],
        name="add",
    )(*gets)
    sent = lax.ppermute(sent, "tm", [(index(a, b, e), index(a, b ^ 1, e)) for a, b, e in every])
    parts = call(
        functools.partial(pair_kernel, nz),
        [shape((3 * step, wrow), F32)] + [shape((3 * step, wrow), B16)] * (nz // 2 - 1),
        [pltpu.VMEM(half.shape, F32)],
        name="pair",
    )(kept, sent)
    parts = [parts[0]] + [over_z(parts[d], 2 * d) for d in range(1, nz // 2)]
    weight_grad, head_grad, loss = call(
        functools.partial(last_kernel, nz // 2),
        [shape((run, 27, block), F32), shape((run, hblock), F32), shape((1, 1), F32)],
        name="last",
    )(*parts)
    return latent.reshape(nf, nrow, ncol, zlat), loss[0, 0], weight_grad.transpose(1, 0, 2), head_grad


def solution(mesh):
    in_specs = (P("tm", "space", None, None), P(), P(), P())
    out_specs = (P("tm", "space", None, None), P(), P(None, "tm", "space"), P("tm", "space"))
    return jax.shard_map(body, mesh=mesh, in_specs=in_specs, out_specs=out_specs, check_vma=False)
```

profile of v0, /device:TPU:32, one launch (start us, length us, event | category | flops | bytes accessed | tf_op | source)
XLA Modules:
  0.0 142.3 jit_solution(16424732435155583391)
XLA Ops:
  0.6 1.7 %first.1 = (bf16[4,24,384]{2,1,0:T(8,128)(2,1)}, bf16[4,24,384]{2,1,0:T(8,128)(2,1)}) custom-call(bf16[4,192,384]{2,1,0:T(8,128)(2,1)} %bitcast.9), custom_call_target="tpu_custom_call" | custom-call | tf_op jit(solution)/shard_map/first/pallas_call | solution.py:391
  2.4 3.4 %collective-permute-start = (bf16[4,24,384]{2,1,0:T(8,128)(2,1)}, bf16[4,24,384]{2,1,0:T(8,128)(2,1)S(1)}, u32[]{:S(2)}, u32[]{:S(2)}) collective-permute-start(bf16[4,24,384]{2,1,0:T(8,128)(2,1)} %get-tuple-element.44), channel_id=1, source_target_pairs={{0,1},{1,2},{2,3},{4,5},{5,6},{6,7},{8,9},{9,10},{10,11},{12,13},{... | collective-permute-start | bytes 221192 | tf_op jit(solution)/shard_map/ppermute | solution.py:393
  8.0 4.2 %collective-permute-done.1.bot_ref = bf16[4,24,384]{2,1,0:T(8,128)(2,1)S(1)} collective-permute-done((bf16[4,24,384]{2,1,0:T(8,128)(2,1)}, bf16[4,24,384]{2,1,0:T(8,128)(2,1)S(1)}, u32[]{:S(2)}, u32[]{:S(2)}) %collective-permute-start.1) | collective-permute-done | bytes 73760 | tf_op jit(solution)/shard_map/ppermute | solution.py:394
  12.2 1.5 %collective-permute-start.3 = (bf16[4,192,384]{2,1,0:T(8,128)(2,1)}, bf16[4,192,384]{2,1,0:T(8,128)(2,1)S(1)}, u32[]{:S(2)}, u32[]{:S(2)}) collective-permute-start(bf16[4,192,384]{2,1,0:T(8,128)(2,1)} %bitcast.10), channel_id=1, source_target_pairs={{0,1},{1,2},{2,3},{3,0},{4,5},{5,6},{6,7},{7,4},{8,9},{9,10},{10,1... | collective-permute-start | bytes 1769480 | tf_op jit(solution)/shard_map/ppermute | solution.py:377
  15.0 2.6 %collective-permute-start.5 = (bf16[4,192,384]{2,1,0:T(8,128)(2,1)}, bf16[4,192,384]{2,1,0:T(8,128)(2,1)S(1)}, u32[]{:S(2)}, u32[]{:S(2)}) collective-permute-start(bf16[4,192,384]{2,1,0:T(8,128)(2,1)} %bitcast.12), channel_id=1, source_target_pairs={{0,3},{1,0},{2,1},{3,2},{4,7},{5,4},{6,5},{7,6},{8,11},{9,8},{10,9... | collective-permute-start | bytes 1769480 | tf_op jit(solution)/shard_map/ppermute | solution.py:377
  17.6 1.9 %ends.1 = bf16[2,240,384]{2,1,0:T(8,128)(2,1)} custom-call(bf16[4,192,384]{2,1,0:T(8,128)(2,1)} %bitcast.13, bf16[4,24,384]{2,1,0:T(8,128)(2,1)} %copy-done.13, bf16[4,24,384]{2,1,0:T(8,128)(2,1)} %copy-done.14), custom_call_target="tpu_custom_call" | custom-call | tf_op jit(solution)/shard_map/ends/pallas_call | solution.py:398
  19.5 1.9 %collective-permute-start.2 = (bf16[2,240,384]{2,1,0:T(8,128)(2,1)}, bf16[2,240,384]{2,1,0:T(8,128)(2,1)S(1)}, u32[]{:S(2)}, u32[]{:S(2)}) collective-permute-start(bf16[2,240,384]{2,1,0:T(8,128)(2,1)} %ends.1), channel_id=1, source_target_pairs={{0,4},{4,8},{8,12},{12,16},{16,20},{20,24},{24,28},{28,32},{32,36}... | collective-permute-start | bytes 1105928 | tf_op jit(solution)/shard_map/ppermute | solution.py:399
  21.4 7.1 %collective-permute-done.2.ends_ref = bf16[2,240,384]{2,1,0:T(8,128)(2,1)S(1)} collective-permute-done((bf16[2,240,384]{2,1,0:T(8,128)(2,1)}, bf16[2,240,384]{2,1,0:T(8,128)(2,1)S(1)}, u32[]{:S(2)}, u32[]{:S(2)}) %collective-permute-start.2) | collective-permute-done | bytes 368672 | tf_op jit(solution)/shard_map/ppermute | solution.py:399
  29.3 14.1 %forward.1 = (f32[768,32]{1,0:T(8,128)}, bf16[128,768]{1,0:T(8,128)(2,1)}, bf16[128,768]{1,0:T(8,128)(2,1)}, bf16[128,768]{1,0:T(8,128)(2,1)}, bf16[128,768]{1,0:T(8,128)(2,1)}) custom-call(s32[21]{0:T(128)} %len_ref.3, bf16[4,192,384]{2,1,0:T(8,128)(2,1)} %bitcast.14, bf16[2,240,384]{2,1,0:T(8,128)(2,1)} %copy-done.12, bf16[4,24,384]{2,1,0:T(8,128)(2,1)} %copy-done.13, ...), custom_call_target="tpu_custom_call" | custom-call | tf_op jit(solution)/shard_map/forward/pallas_call | solution.py:406
  43.5 1.7 %collective-permute-start.7 = (bf16[128,768]{1,0:T(8,128)(2,1)}, bf16[128,768]{1,0:T(8,128)(2,1)S(1)}, u32[]{:S(2)}, u32[]{:S(2)}) collective-permute-start(bf16[128,768]{1,0:T(8,128)(2,1)} %get-tuple-element.56), channel_id=1, source_target_pairs={{0,2},{1,3},{2,0},{3,1},{4,6},{5,7},{6,4},{7,5},{8,10},{9,11},{10,... | collective-permute-start | bytes 589832 | tf_op jit(solution)/shard_map/ppermute | solution.py:377
  45.2 1.7 %collective-permute-start.8 = (bf16[128,768]{1,0:T(8,128)(2,1)}, bf16[128,768]{1,0:T(8,128)(2,1)S(1)}, u32[]{:S(2)}, u32[]{:S(2)}) collective-permute-start(bf16[128,768]{1,0:T(8,128)(2,1)} %get-tuple-element.57), channel_id=1, source_target_pairs={{0,3},{1,0},{2,1},{3,2},{4,7},{5,4},{6,5},{7,6},{8,11},{9,8},{10,9... | collective-permute-start | bytes 589832 | tf_op jit(solution)/shard_map/ppermute | solution.py:377
  47.0 5.6 %choose.1 = (bf16[4,768,256]{2,1,0:T(8,128)(2,1)}, bf16[4,768,256]{2,1,0:T(8,128)(2,1)}) custom-call(bf16[4,192,384]{2,1,0:T(8,128)(2,1)} %bitcast.15, bf16[4,192,384]{2,1,0:T(8,128)(2,1)} %copy-done.9, bf16[4,192,384]{2,1,0:T(8,128)(2,1)} %copy-done.10, bf16[4,192,384]{2,1,0:T(8,128)(2,1)} %copy-done.11, bf16[2,384,512]{2,1,0:T(8,128)(2,1)} %constant.2.clone.table_ref), custom_call_target="tpu_custom_call" | custom-call | tf_op jit(solution)/shard_map/choose/pallas_call | solution.py:428
  52.6 3.0 %collective-permute-done.6.refs_1_.a1 = bf16[128,768]{1,0:T(8,128)(2,1)S(1)} collective-permute-done((bf16[128,768]{1,0:T(8,128)(2,1)}, bf16[128,768]{1,0:T(8,128)(2,1)S(1)}, u32[]{:S(2)}, u32[]{:S(2)}) %collective-permute-start.6) | collective-permute-done | bytes 196640 | tf_op jit(solution)/shard_map/ppermute | solution.py:377
  57.3 2.3 %collective-permute-done.10.refs_5_.b1 = bf16[128,768]{1,0:T(8,128)(2,1)S(1)} collective-permute-done((bf16[128,768]{1,0:T(8,128)(2,1)S(1)}, bf16[128,768]{1,0:T(8,128)(2,1)S(1)}, u32[]{:S(2)}, u32[]{:S(2)}) %collective-permute-start.10) | collective-permute-done | bytes 196640 | tf_op jit(solution)/shard_map/ppermute | solution.py:371
  61.5 2.0 %clip.1 = (f32[8,128]{1,0:T(8,128)}, bf16[4,96,384]{2,1,0:T(8,128)(2,1)}) custom-call(bf16[128,768]{1,0:T(8,128)(2,1)} %get-tuple-element.63.refs_0_.a0, bf16[128,768]{1,0:T(8,128)(2,1)} %copy-done.2, bf16[128,768]{1,0:T(8,128)(2,1)} %copy-done.3, bf16[128,768]{1,0:T(8,128)(2,1)} %copy-done.4, bf16[128,768]{1,0:T(8,128)(2,1)} %copy-done.8, ...), custom_call_target="tpu_custom_call" | custom-call | tf_op jit(solution)/shard_map/clip/pallas_call | solution.py:442
  63.5 2.0 %collective-permute-start.13 = (f32[8,128]{1,0:T(8,128)}, f32[8,128]{1,0:T(8,128)S(1)}, u32[]{:S(2)}, u32[]{:S(2)}) collective-permute-start(f32[8,128]{1,0:T(8,128)} %get-tuple-element.67.mid_ref), channel_id=1, source_target_pairs={{0,8},{4,12},{8,16},{12,20},{16,24},{20,28},{24,32},{28,36},{32,40... | collective-permute-start | bytes 12296 | tf_op jit(solution)/shard_map/ppermute | solution.py:374
  65.5 4.9 %collective-permute-start.14 = (f32[8,128]{1,0:T(8,128)}, f32[8,128]{1,0:T(8,128)S(1)}, u32[]{:S(2)}, u32[]{:S(2)}) collective-permute-start(f32[8,128]{1,0:T(8,128)} %get-tuple-element.67.mid_ref), channel_id=1, source_target_pairs={{0,248},{4,252},{8,0},{12,4},{16,8},{20,12},{24,16},{28,20},{32,24... | collective-permute-start | bytes 12296 | tf_op jit(solution)/shard_map/ppermute | solution.py:374
  70.4 1.8 %collective-permute-done.13 = f32[8,128]{1,0:T(8,128)S(1)} collective-permute-done((f32[8,128]{1,0:T(8,128)}, f32[8,128]{1,0:T(8,128)S(1)}, u32[]{:S(2)}, u32[]{:S(2)}) %collective-permute-start.13) | collective-permute-done | bytes 4128 | tf_op jit(solution)/shard_map/ppermute | solution.py:374
  73.9 5.5 %collective-permute-start.15 = (f32[3,8,128]{2,1,0:T(8,128)S(1)}, f32[3,8,128]{2,1,0:T(8,128)S(1)}, u32[]{:S(2)}, u32[]{:S(2)}) collective-permute-start(f32[3,8,128]{2,1,0:T(8,128)S(1)} %pad_maximum_fusion), channel_id=1, source_target_pairs={{0,16},{4,20},{8,24},{12,28},{16,32},{20,36},{24,40},{28,44},{32,4... | collective-permute-start | bytes 36872 | tf_op jit(solution)/shard_map/ppermute | solution.py:374
  79.4 3.9 %collective-permute-start.16 = (f32[3,8,128]{2,1,0:T(8,128)S(1)}, f32[3,8,128]{2,1,0:T(8,128)S(1)}, u32[]{:S(2)}, u32[]{:S(2)}) collective-permute-start(f32[3,8,128]{2,1,0:T(8,128)S(1)} %pad_maximum_fusion), channel_id=1, source_target_pairs={{0,240},{4,244},{8,248},{12,252},{16,0},{20,4},{24,8},{28,12},{32,... | collective-permute-start | bytes 36872 | tf_op jit(solution)/shard_map/ppermute | solution.py:374
  83.4 1.7 %collective-permute-done.15.left_ref = f32[3,8,128]{2,1,0:T(8,128)S(1)} collective-permute-done((f32[3,8,128]{2,1,0:T(8,128)S(1)}, f32[3,8,128]{2,1,0:T(8,128)S(1)}, u32[]{:S(2)}, u32[]{:S(2)}) %collective-permute-start.15) | collective-permute-done | bytes 12320 | tf_op jit(solution)/shard_map/ppermute | solution.py:374
  86.3 15.6 %weight.1 = (f32[3,48,896]{2,1,0:T(8,128)}, bf16[3,48,896]{2,1,0:T(8,128)(2,1)}, bf16[3,48,896]{2,1,0:T(8,128)(2,1)}, bf16[3,48,896]{2,1,0:T(8,128)(2,1)}) custom-call(s32[21]{0:T(128)} %len_ref.3, f32[3,8,128]{2,1,0:T(8,128)} %copy-done.23, f32[8,128]{1,0:T(8,128)} %get-tuple-element.67.mid_ref, f32[3,8,128]{2,1,0:T(8,128)} %copy-done.24, ...), custom_call_target="tpu_custom_call" | custom-call | tf_op jit(solution)/shard_map/weight/pallas_call | solution.py:456
  102.6 2.9 %collective-permute-start.20 = (bf16[3,48,896]{2,1,0:T(8,128)(2,1)}, bf16[3,48,896]{2,1,0:T(8,128)(2,1)S(1)}, u32[]{:S(2)}, u32[]{:S(2)}) collective-permute-start(bf16[3,48,896]{2,1,0:T(8,128)(2,1)} %get-tuple-element.73), channel_id=1, source_target_pairs={{0,128},{4,132},{8,136},{12,140},{16,144},{20,148},{24,152},{28,15... | collective-permute-start | bytes 774152 | tf_op jit(solution)/shard_map/ppermute | solution.py:380
  105.5 1.3 collective-permute-start.21
  106.8 9.0 %collective-permute-done.19.refs_1_ = bf16[3,48,896]{2,1,0:T(8,128)(2,1)S(1)} collective-permute-done((bf16[3,48,896]{2,1,0:T(8,128)(2,1)}, bf16[3,48,896]{2,1,0:T(8,128)(2,1)S(1)}, u32[]{:S(2)}, u32[]{:S(2)}) %collective-permute-start.19) | collective-permute-done | bytes 258080 | tf_op jit(solution)/shard_map/ppermute | solution.py:380
  117.1 2.5 %add.1 = (f32[4,24,896]{2,1,0:T(8,128)}, bf16[4,24,896]{2,1,0:T(8,128)(2,1)}) custom-call(f32[3,48,896]{2,1,0:T(8,128)} %get-tuple-element.71.refs_0_, bf16[3,48,896]{2,1,0:T(8,128)(2,1)} %copy-done.16, bf16[3,48,896]{2,1,0:T(8,128)(2,1)} %copy-done.17, bf16[3,48,896]{2,1,0:T(8,128)(2,1)} %copy-done.18), custom_call_target="tpu_custom_call" | custom-call | tf_op jit(solution)/shard_map/add/pallas_call | solution.py:476
  120.3 4.9 %collective-permute-done.22.got_ref = bf16[4,24,896]{2,1,0:T(8,128)(2,1)S(1)} collective-permute-done((bf16[4,24,896]{2,1,0:T(8,128)(2,1)}, bf16[4,24,896]{2,1,0:T(8,128)(2,1)S(1)}, u32[]{:S(2)}, u32[]{:S(2)}) %collective-permute-start.22) | collective-permute-done | bytes 172064 | tf_op jit(solution)/shard_map/ppermute | solution.py:482
  125.9 1.7 %pair.1 = (f32[24,896]{1,0:T(8,128)}, bf16[24,896]{1,0:T(8,128)(2,1)}, bf16[24,896]{1,0:T(8,128)(2,1)}, bf16[24,896]{1,0:T(8,128)(2,1)}) custom-call(f32[4,24,896]{2,1,0:T(8,128)} %get-tuple-element.75.keep_ref, bf16[4,24,896]{2,1,0:T(8,128)(2,1)} %copy-done.19), custom_call_target="tpu_custom_call" | custom-call | tf_op jit(solution)/shard_map/pair/pallas_call | solution.py:483
  128.5 5.7 %collective-permute-start.24 = (bf16[24,896]{1,0:T(8,128)(2,1)}, bf16[24,896]{1,0:T(8,128)(2,1)S(1)}, u32[]{:S(2)}, u32[]{:S(2)}) collective-permute-start(bf16[24,896]{1,0:T(8,128)(2,1)} %get-tuple-element.79), channel_id=1, source_target_pairs={{0,32},{4,36},{8,40},{12,44},{16,48},{20,52},{24,56},{28,60},{32,0... | collective-permute-start | bytes 129032 | tf_op jit(solution)/shard_map/ppermute | solution.py:383
  134.8 2.0 %collective-permute-done.24.refs_2_ = bf16[24,896]{1,0:T(8,128)(2,1)S(1)} collective-permute-done((bf16[24,896]{1,0:T(8,128)(2,1)}, bf16[24,896]{1,0:T(8,128)(2,1)S(1)}, u32[]{:S(2)}, u32[]{:S(2)}) %collective-permute-start.24) | collective-permute-done | bytes 43040 | tf_op jit(solution)/shard_map/ppermute | solution.py:383
  136.8 3.0 %collective-permute-done.25.refs_3_ = bf16[24,896]{1,0:T(8,128)(2,1)S(1)} collective-permute-done((bf16[24,896]{1,0:T(8,128)(2,1)}, bf16[24,896]{1,0:T(8,128)(2,1)S(1)}, u32[]{:S(2)}, u32[]{:S(2)}) %collective-permute-start.25) | collective-permute-done | bytes 43040 | tf_op jit(solution)/shard_map/ppermute | solution.py:383
  140.4 1.8 %last.1 = (f32[6,27,96]{2,1,0:T(8,128)}, f32[6,8]{1,0:T(8,128)}, f32[1,1]{1,0:T(1,128)}) custom-call(f32[24,896]{1,0:T(8,128)} %get-tuple-element.77.refs_0_, bf16[24,896]{1,0:T(8,128)(2,1)} %copy-done.20, bf16[24,896]{1,0:T(8,128)(2,1)} %copy-done.21, bf16[24,896]{1,0:T(8,128)(2,1)} %copy-done.22), custom_call_target="tpu_custom_call" | custom-call | tf_op jit(solution)/shard_map/last/pallas_call | solution.py:490
  (80 shorter events, 16.4 us)
Async XLA Ops:
  2.4 5.7 %collective-permute-start = (bf16[4,24,384]{2,1,0:T(8,128)(2,1)}, bf16[4,24,384]{2,1,0:T(8,128)(2,1)S(1)}, u32[]{:S(2)}, u32[]{:S(2)}) collective-permute-start(bf16[4,24,384]{2,1,0:T(8,128)(2,1)} %get-tuple-element.44), channel_id=1, source_target_pairs={{0,1},{1,2},{2,3},{4,5},{5,6},{6,7},{8,9},{9,10},{10,11},{12,13},{... | collective-permute-start | bytes 221192 | tf_op jit(solution)/shard_map/ppermute | solution.py:393
  5.8 6.5 %collective-permute-start.1 = (bf16[4,24,384]{2,1,0:T(8,128)(2,1)}, bf16[4,24,384]{2,1,0:T(8,128)(2,1)S(1)}, u32[]{:S(2)}, u32[]{:S(2)}) collective-permute-start(bf16[4,24,384]{2,1,0:T(8,128)(2,1)} %get-tuple-element.45), channel_id=1, source_target_pairs={{1,0},{2,1},{3,2},{5,4},{6,5},{7,6},{9,8},{10,9},{11,10},{13,12},{... | collective-permute-start | bytes 221192 | tf_op jit(solution)/shard_map/ppermute | solution.py:394
  8.0 9.5 %copy-start.13 = (bf16[4,24,384]{2,1,0:T(8,128)(2,1)}, bf16[4,24,384]{2,1,0:T(8,128)(2,1)S(1)}, u32[]{:S(2)}) copy-start(bf16[4,24,384]{2,1,0:T(8,128)(2,1)S(1)} %collective-permute-done.top_ref) | copy-start | bytes 221188
  12.2 5.4 %copy-start.14 = (bf16[4,24,384]{2,1,0:T(8,128)(2,1)}, bf16[4,24,384]{2,1,0:T(8,128)(2,1)S(1)}, u32[]{:S(2)}) copy-start(bf16[4,24,384]{2,1,0:T(8,128)(2,1)S(1)} %collective-permute-done.1.bot_ref) | copy-start | bytes 221188
  12.2 31.2 %collective-permute-start.3 = (bf16[4,192,384]{2,1,0:T(8,128)(2,1)}, bf16[4,192,384]{2,1,0:T(8,128)(2,1)S(1)}, u32[]{:S(2)}, u32[]{:S(2)}) collective-permute-start(bf16[4,192,384]{2,1,0:T(8,128)(2,1)} %bitcast.10), channel_id=1, source_target_pairs={{0,1},{1,2},{2,3},{3,0},{4,5},{5,6},{6,7},{7,4},{8,9},{9,10},{10,1... | collective-permute-start | bytes 1769480 | tf_op jit(solution)/shard_map/ppermute | solution.py:377
  13.7 29.7 %collective-permute-start.4 = (bf16[4,192,384]{2,1,0:T(8,128)(2,1)}, bf16[4,192,384]{2,1,0:T(8,128)(2,1)S(1)}, u32[]{:S(2)}, u32[]{:S(2)}) collective-permute-start(bf16[4,192,384]{2,1,0:T(8,128)(2,1)} %bitcast.11), channel_id=1, source_target_pairs={{0,2},{1,3},{2,0},{3,1},{4,6},{5,7},{6,4},{7,5},{8,10},{9,11},{10,... | collective-permute-start | bytes 1769480 | tf_op jit(solution)/shard_map/ppermute | solution.py:377
  15.0 28.5 %collective-permute-start.5 = (bf16[4,192,384]{2,1,0:T(8,128)(2,1)}, bf16[4,192,384]{2,1,0:T(8,128)(2,1)S(1)}, u32[]{:S(2)}, u32[]{:S(2)}) collective-permute-start(bf16[4,192,384]{2,1,0:T(8,128)(2,1)} %bitcast.12), channel_id=1, source_target_pairs={{0,3},{1,0},{2,1},{3,2},{4,7},{5,4},{6,5},{7,6},{8,11},{9,8},{10,9... | collective-permute-start | bytes 1769480 | tf_op jit(solution)/shard_map/ppermute | solution.py:377
  19.5 9.0 %collective-permute-start.2 = (bf16[2,240,384]{2,1,0:T(8,128)(2,1)}, bf16[2,240,384]{2,1,0:T(8,128)(2,1)S(1)}, u32[]{:S(2)}, u32[]{:S(2)}) collective-permute-start(bf16[2,240,384]{2,1,0:T(8,128)(2,1)} %ends.1), channel_id=1, source_target_pairs={{0,4},{4,8},{8,12},{12,16},{16,20},{20,24},{24,28},{28,32},{32,36}... | collective-permute-start | bytes 1105928 | tf_op jit(solution)/shard_map/ppermute | solution.py:399
  43.4 13.8 %copy-start.1 = (bf16[128,768]{1,0:T(8,128)(2,1)S(1)}, bf16[128,768]{1,0:T(8,128)(2,1)}, u32[]{:S(2)}) copy-start(bf16[128,768]{1,0:T(8,128)(2,1)} %get-tuple-element.63.refs_0_.a0) | copy-start | bytes 589828
  43.5 12.2 %collective-permute-start.6 = (bf16[128,768]{1,0:T(8,128)(2,1)}, bf16[128,768]{1,0:T(8,128)(2,1)S(1)}, u32[]{:S(2)}, u32[]{:S(2)}) collective-permute-start(bf16[128,768]{1,0:T(8,128)(2,1)} %get-tuple-element.55), channel_id=1, source_target_pairs={{0,1},{1,2},{2,3},{3,0},{4,5},{5,6},{6,7},{7,4},{8,9},{9,10},{10,1... | collective-permute-start | bytes 589832 | tf_op jit(solution)/shard_map/ppermute | solution.py:377
  43.5 12.1 %collective-permute-start.7 = (bf16[128,768]{1,0:T(8,128)(2,1)}, bf16[128,768]{1,0:T(8,128)(2,1)S(1)}, u32[]{:S(2)}, u32[]{:S(2)}) collective-permute-start(bf16[128,768]{1,0:T(8,128)(2,1)} %get-tuple-element.56), channel_id=1, source_target_pairs={{0,2},{1,3},{2,0},{3,1},{4,6},{5,7},{6,4},{7,5},{8,10},{9,11},{10,... | collective-permute-start | bytes 589832 | tf_op jit(solution)/shard_map/ppermute | solution.py:377
  45.2 11.0 %collective-permute-start.8 = (bf16[128,768]{1,0:T(8,128)(2,1)}, bf16[128,768]{1,0:T(8,128)(2,1)S(1)}, u32[]{:S(2)}, u32[]{:S(2)}) collective-permute-start(bf16[128,768]{1,0:T(8,128)(2,1)} %get-tuple-element.57), channel_id=1, source_target_pairs={{0,3},{1,0},{2,1},{3,2},{4,7},{5,4},{6,5},{7,6},{8,11},{9,8},{10,9... | collective-permute-start | bytes 589832 | tf_op jit(solution)/shard_map/ppermute | solution.py:377
  55.6 4.8 %copy-start.2 = (bf16[128,768]{1,0:T(8,128)(2,1)}, bf16[128,768]{1,0:T(8,128)(2,1)S(1)}, u32[]{:S(2)}) copy-start(bf16[128,768]{1,0:T(8,128)(2,1)S(1)} %collective-permute-done.6.refs_1_.a1) | copy-start | bytes 589828
  55.6 4.8 %copy-start.3 = (bf16[128,768]{1,0:T(8,128)(2,1)}, bf16[128,768]{1,0:T(8,128)(2,1)S(1)}, u32[]{:S(2)}) copy-start(bf16[128,768]{1,0:T(8,128)(2,1)S(1)} %collective-permute-done.7.refs_2_.a2) | copy-start | bytes 589828
  56.3 28.8 %collective-permute-start.18 = (bf16[4,768,256]{2,1,0:T(8,128)(2,1)}, bf16[4,768,256]{2,1,0:T(8,128)(2,1)S(1)}, u32[]{:S(2)}, u32[]{:S(2)}) collective-permute-start(bf16[4,768,256]{2,1,0:T(8,128)(2,1)} %get-tuple-element.70), channel_id=1, source_target_pairs={{0,4},{4,0},{8,12},{12,8},{16,20},{20,16},{24,28},{28,24},{32,36},... | collective-permute-start | bytes 4718600 | tf_op jit(solution)/shard_map/ppermute | solution.py:371
  56.3 3.3 %collective-permute-start.10 = (bf16[128,768]{1,0:T(8,128)(2,1)S(1)}, bf16[128,768]{1,0:T(8,128)(2,1)S(1)}, u32[]{:S(2)}, u32[]{:S(2)}) collective-permute-start(bf16[128,768]{1,0:T(8,128)(2,1)S(1)} %collective-permute-done.6.refs_1_.a1), channel_id=1, source_target_pairs={{0,4},{4,0},{8,12},{12,8},{16,20},{20,16},{24,28},{28,24},{32,36},... | collective-permute-start | bytes 589832 | tf_op jit(solution)/shard_map/ppermute | solution.py:371
  56.8 3.1 %collective-permute-start.11 = (bf16[128,768]{1,0:T(8,128)(2,1)S(1)}, bf16[128,768]{1,0:T(8,128)(2,1)S(1)}, u32[]{:S(2)}, u32[]{:S(2)}) collective-permute-start(bf16[128,768]{1,0:T(8,128)(2,1)S(1)} %collective-permute-done.7.refs_2_.a2), channel_id=1, source_target_pairs={{0,4},{4,0},{8,12},{12,8},{16,20},{20,16},{24,28},{28,24},{32,36},... | collective-permute-start | bytes 589832 | tf_op jit(solution)/shard_map/ppermute | solution.py:371
  56.8 3.4 %collective-permute-start.12 = (bf16[128,768]{1,0:T(8,128)(2,1)S(1)}, bf16[128,768]{1,0:T(8,128)(2,1)S(1)}, u32[]{:S(2)}, u32[]{:S(2)}) collective-permute-start(bf16[128,768]{1,0:T(8,128)(2,1)S(1)} %collective-permute-done.8.refs_3_.a3), channel_id=1, source_target_pairs={{0,4},{4,0},{8,12},{12,8},{16,20},{20,16},{24,28},{28,24},{32,36},... | collective-permute-start | bytes 589832 | tf_op jit(solution)/shard_map/ppermute | solution.py:371
  57.3 3.1 %collective-permute-start.9 = (bf16[128,768]{1,0:T(8,128)(2,1)S(1)}, bf16[128,768]{1,0:T(8,128)(2,1)S(1)}, u32[]{:S(2)}, u32[]{:S(2)}) collective-permute-start(bf16[128,768]{1,0:T(8,128)(2,1)S(1)} %copy-done.1), channel_id=1, source_target_pairs={{0,4},{4,0},{8,12},{12,8},{16,20},{20,16},{24,28},{28,24},{32,36},... | collective-permute-start | bytes 589832 | tf_op jit(solution)/shard_map/ppermute | solution.py:371
  63.5 21.6 %collective-permute-start.17 = (bf16[4,96,384]{2,1,0:T(8,128)(2,1)}, bf16[4,96,384]{2,1,0:T(8,128)(2,1)S(1)}, u32[]{:S(2)}, u32[]{:S(2)}) collective-permute-start(bf16[4,96,384]{2,1,0:T(8,128)(2,1)} %get-tuple-element.68), channel_id=1, source_target_pairs={{0,248},{4,252},{8,0},{12,4},{16,8},{20,12},{24,16},{28,20},{32,24... | collective-permute-start | bytes 884744 | tf_op jit(solution)/shard_map/ppermute | solution.py:374
  63.5 8.7 %collective-permute-start.13 = (f32[8,128]{1,0:T(8,128)}, f32[8,128]{1,0:T(8,128)S(1)}, u32[]{:S(2)}, u32[]{:S(2)}) collective-permute-start(f32[8,128]{1,0:T(8,128)} %get-tuple-element.67.mid_ref), channel_id=1, source_target_pairs={{0,8},{4,12},{8,16},{12,20},{16,24},{20,28},{24,32},{28,36},{32,40... | collective-permute-start | bytes 12296 | tf_op jit(solution)/shard_map/ppermute | solution.py:374
  65.5 7.7 %collective-permute-start.14 = (f32[8,128]{1,0:T(8,128)}, f32[8,128]{1,0:T(8,128)S(1)}, u32[]{:S(2)}, u32[]{:S(2)}) collective-permute-start(f32[8,128]{1,0:T(8,128)} %get-tuple-element.67.mid_ref), channel_id=1, source_target_pairs={{0,248},{4,252},{8,0},{12,4},{16,8},{20,12},{24,16},{28,20},{32,24... | collective-permute-start | bytes 12296 | tf_op jit(solution)/shard_map/ppermute | solution.py:374
  73.9 11.1 %collective-permute-start.15 = (f32[3,8,128]{2,1,0:T(8,128)S(1)}, f32[3,8,128]{2,1,0:T(8,128)S(1)}, u32[]{:S(2)}, u32[]{:S(2)}) collective-permute-start(f32[3,8,128]{2,1,0:T(8,128)S(1)} %pad_maximum_fusion), channel_id=1, source_target_pairs={{0,16},{4,20},{8,24},{12,28},{16,32},{20,36},{24,40},{28,44},{32,4... | collective-permute-start | bytes 36872 | tf_op jit(solution)/shard_map/ppermute | solution.py:374
  79.4 5.6 %collective-permute-start.16 = (f32[3,8,128]{2,1,0:T(8,128)S(1)}, f32[3,8,128]{2,1,0:T(8,128)S(1)}, u32[]{:S(2)}, u32[]{:S(2)}) collective-permute-start(f32[3,8,128]{2,1,0:T(8,128)S(1)} %pad_maximum_fusion), channel_id=1, source_target_pairs={{0,240},{4,244},{8,248},{12,252},{16,0},{20,4},{24,8},{28,12},{32,... | collective-permute-start | bytes 36872 | tf_op jit(solution)/shard_map/ppermute | solution.py:374
  101.9 13.8 %collective-permute-start.19 = (bf16[3,48,896]{2,1,0:T(8,128)(2,1)}, bf16[3,48,896]{2,1,0:T(8,128)(2,1)S(1)}, u32[]{:S(2)}, u32[]{:S(2)}) collective-permute-start(bf16[3,48,896]{2,1,0:T(8,128)(2,1)} %get-tuple-element.72), channel_id=1, source_target_pairs={{0,64},{4,68},{8,72},{12,76},{16,80},{20,84},{24,88},{28,92},{32,9... | collective-permute-start | bytes 774152 | tf_op jit(solution)/shard_map/ppermute | solution.py:380
  102.6 13.2 %collective-permute-start.20 = (bf16[3,48,896]{2,1,0:T(8,128)(2,1)}, bf16[3,48,896]{2,1,0:T(8,128)(2,1)S(1)}, u32[]{:S(2)}, u32[]{:S(2)}) collective-permute-start(bf16[3,48,896]{2,1,0:T(8,128)(2,1)} %get-tuple-element.73), channel_id=1, source_target_pairs={{0,128},{4,132},{8,136},{12,140},{16,144},{20,148},{24,152},{28,15... | collective-permute-start | bytes 774152 | tf_op jit(solution)/shard_map/ppermute | solution.py:380
  105.5 10.9 %collective-permute-start.21 = (bf16[3,48,896]{2,1,0:T(8,128)(2,1)}, bf16[3,48,896]{2,1,0:T(8,128)(2,1)S(1)}, u32[]{:S(2)}, u32[]{:S(2)}) collective-permute-start(bf16[3,48,896]{2,1,0:T(8,128)(2,1)} %get-tuple-element.74), channel_id=1, source_target_pairs={{0,192},{4,196},{8,200},{12,204},{16,208},{20,212},{24,216},{28,22... | collective-permute-start | bytes 774152 | tf_op jit(solution)/shard_map/ppermute | solution.py:380
  119.6 5.6 %collective-permute-start.22 = (bf16[4,24,896]{2,1,0:T(8,128)(2,1)}, bf16[4,24,896]{2,1,0:T(8,128)(2,1)S(1)}, u32[]{:S(2)}, u32[]{:S(2)}) collective-permute-start(bf16[4,24,896]{2,1,0:T(8,128)(2,1)} %get-tuple-element.76), channel_id=1, source_target_pairs={{0,8},{4,12},{8,0},{12,4},{16,24},{20,28},{24,16},{28,20},{32,40},... | collective-permute-start | bytes 516104 | tf_op jit(solution)/shard_map/ppermute | solution.py:482
  127.6 7.1 %collective-permute-start.23 = (bf16[24,896]{1,0:T(8,128)(2,1)}, bf16[24,896]{1,0:T(8,128)(2,1)S(1)}, u32[]{:S(2)}, u32[]{:S(2)}) collective-permute-start(bf16[24,896]{1,0:T(8,128)(2,1)} %get-tuple-element.78), channel_id=1, source_target_pairs={{0,16},{4,20},{8,24},{12,28},{16,32},{20,36},{24,40},{28,44},{32,4... | collective-permute-start | bytes 129032 | tf_op jit(solution)/shard_map/ppermute | solution.py:383
  128.5 8.2 %collective-permute-start.24 = (bf16[24,896]{1,0:T(8,128)(2,1)}, bf16[24,896]{1,0:T(8,128)(2,1)S(1)}, u32[]{:S(2)}, u32[]{:S(2)}) collective-permute-start(bf16[24,896]{1,0:T(8,128)(2,1)} %get-tuple-element.79), channel_id=1, source_target_pairs={{0,32},{4,36},{8,40},{12,44},{16,48},{20,52},{24,56},{28,60},{32,0... | collective-permute-start | bytes 129032 | tf_op jit(solution)/shard_map/ppermute | solution.py:383
  134.2 5.6 %collective-permute-start.25 = (bf16[24,896]{1,0:T(8,128)(2,1)}, bf16[24,896]{1,0:T(8,128)(2,1)S(1)}, u32[]{:S(2)}, u32[]{:S(2)}) collective-permute-start(bf16[24,896]{1,0:T(8,128)(2,1)} %get-tuple-element.80), channel_id=1, source_target_pairs={{0,48},{4,52},{8,56},{12,60},{16,0},{20,4},{24,8},{28,12},{32,16},... | collective-permute-start | bytes 129032 | tf_op jit(solution)/shard_map/ppermute | solution.py:383
  134.8 5.1 %copy-start.20 = (bf16[24,896]{1,0:T(8,128)(2,1)}, bf16[24,896]{1,0:T(8,128)(2,1)S(1)}, u32[]{:S(2)}) copy-start(bf16[24,896]{1,0:T(8,128)(2,1)S(1)} %collective-permute-done.23.refs_1_) | copy-start | bytes 129028
  (19 other events, 28.2 us)
where the time goes:
time: 143 us; the launch traced here: 142 us
  Pallas kernels  47 us (33%)
  starting transfers between devices  45.6 us (32%)
  waiting for transfers between devices  43.1 us (30%)
  local copies, waits for them, and re-layouts  5.08 us (4%)
    ppermute x5, starting transfers between devices, over_chip(): lax.ppermute(v, 'tm', [(i, (i + 2 * d) % count) for i in range(count)])  16.4 us
    pallas_call x1, Pallas kernels, body(): call(functools.partial(weight_kernel, ny, nz, float(4 * band)), [shape((3...  15.6 us
    pallas_call x1, Pallas kernels, body(): call(forward_kernel, [shape((cells, zlat), F32)] + [message] * 4, [pltpu....  14.1 us
    ppermute x3, waiting for transfers between devices, over_y(): lax.ppermute(v, 'tm', [(index(a, b, e), index(a + d, b, e)) for a, b, e i...  9.58 us
    ppermute x6, starting transfers between devices, over_x(): return lax.ppermute(v, 'space', [(i, (i + d) % 4) for i in range(4)])  8.87 us
    ppermute x3, starting transfers between devices, over_z(): lax.ppermute(v, 'tm', [(index(a, b, e), index(a, b + d, e)) for a, b, e i...  7.14 us
    ppermute x1, waiting for transfers between devices, body(): ends = lax.ppermute(ends, 'tm', [(i, i + 1) for i in range(count - 1)])  7.11 us
    pallas_call x1, Pallas kernels, body(): call(choose_kernel, [chosen, chosen], [pltpu.VMEM((4 * band, chans), B16)...  5.62 us
  transfers between devices with their start and end apart: 26, of which 17 were waited for; matrix products, arithmetic and copies ran while one was open for 0% of the time, Pallas kernels for 17%

commit v1 on v0

--- a/solution.py
+++ b/solution.py
@@ -94,7 +94,8 @@
     for load in loads:
         load.start()
     col = lax.rem(lax.broadcasted_iota(jnp.int32, (rows, 1), 0), COLS)
-    for f in range(nf + 2):
+
+    def build(f):
         if f < 2:
             v = ends_ref[f].astype(F32)
         else:
@@ -119,7 +120,11 @@
         for f in range(nf):
             pos[f] = jnp.where(t * nf + f >= start, t * nf + f - start, pos[f])
         start = start + len_ref[j]
+    for f in range(nf):
+        build(f)
     for dt in range(3):
+        if dt:
+            build(nf - 1 + dt)
         loads[dt].wait()
         part = dot(wide_ref[dt * band : (dt + nf) * band, :], held_ref[dt])
         for f in range(nf):
@@ -447,8 +452,10 @@
         out_specs=[whole(chip, 128), whole(4, block, 2 * band)],
         name="clip",
     )(*mine_d, *core_d)
+    before, after = over_chip(kchip, 1), over_chip(kchip, -1)
+    tail, before, after = lax.optimization_barrier((tail, before, after))
     tail = over_chip(tail, -1)
-    triple = jnp.stack([over_chip(kchip, 1), kchip, over_chip(kchip, -1)])
+    triple = jnp.stack([before, kchip, after])
     left, right = over_chip(triple, 2), over_chip(triple, -2)
 
     rows = run * nz

time: 143 us -> 142 us (level)
  starting transfers between devices: 45.6 us -> 43.4 us
    ppermute x5, starting transfers between devices: 16.4 us -> 9.87 us  [over_chip(): lax.ppermute(v, 'tm', [(i, (i + 2 * d) % count) for i in range(count)])]
    ppermute x1, starting transfers between devices: 0.74 us -> 4.33 us  [body(): lax.ppermute(sent, 'tm', [(index(a, b, e), index(a, b ^ 1, e)) for a, b,...]
    ppermute x5, waiting for transfers between devices: 4.53 us -> 6.61 us  [over_chip(): lax.ppermute(v, 'tm', [(i, (i + 2 * d) % count) for i in range(count)])]
  transfers between devices with their start and end apart: 26 -> 26, of which waited for: 17 -> 19; matrix products, arithmetic and copies ran while one was open for 0% -> 0% of each run, Pallas kernels for 17% -> 17%
where the time goes in v1:
time: 142 us; the launch traced here: 140 us
  Pallas kernels  47.4 us (33%)
  starting transfers between devices  43.4 us (31%)
  waiting for transfers between devices  42.8 us (30%)
  local copies, waits for them, and re-layouts  5.21 us (4%)
    pallas_call x1, Pallas kernels, body(): call(functools.partial(weight_kernel, ny, nz, float(4 * band)), [shape((3...  15.6 us
    pallas_call x1, Pallas kernels, body(): call(forward_kernel, [shape((cells, zlat), F32)] + [message] * 4, [pltpu....  14.5 us
    ppermute x5, starting transfers between devices, over_chip(): lax.ppermute(v, 'tm', [(i, (i + 2 * d) % count) for i in range(count)])  9.87 us
    ppermute x6, starting transfers between devices, over_x(): return lax.ppermute(v, 'space', [(i, (i + d) % 4) for i in range(4)])  8.86 us
    ppermute x3, waiting for transfers between devices, over_y(): lax.ppermute(v, 'tm', [(index(a, b, e), index(a + d, b, e)) for a, b, e i...  8.47 us
    ppermute x1, waiting for transfers between devices, body(): ends = lax.ppermute(ends, 'tm', [(i, i + 1) for i in range(count - 1)])  7.11 us
    ppermute x3, starting transfers between devices, over_z(): lax.ppermute(v, 'tm', [(index(a, b, e), index(a, b + d, e)) for a, b, e i...  6.8 us
    ppermute x5, waiting for transfers between devices, over_chip(): lax.ppermute(v, 'tm', [(i, (i + 2 * d) % count) for i in range(count)])  6.61 us
  transfers between devices with their start and end apart: 26, of which 19 were waited for; matrix products, arithmetic and copies ran while one was open for 0% of the time, Pallas kernels for 17%

profile of v1, /device:TPU:32, one launch (start us, length us, event | category | flops | bytes accessed | tf_op | source)
XLA Modules:
  0.0 140.3 jit_solution(17757032141081914704)
XLA Ops:
  0.6 1.7 %first.1 = (bf16[4,24,384]{2,1,0:T(8,128)(2,1)}, bf16[4,24,384]{2,1,0:T(8,128)(2,1)}) custom-call(bf16[4,192,384]{2,1,0:T(8,128)(2,1)} %bitcast.9), custom_call_target="tpu_custom_call" | custom-call | tf_op jit(solution)/shard_map/first/pallas_call | solution.py:396
  2.4 3.4 %collective-permute-start = (bf16[4,24,384]{2,1,0:T(8,128)(2,1)}, bf16[4,24,384]{2,1,0:T(8,128)(2,1)S(1)}, u32[]{:S(2)}, u32[]{:S(2)}) collective-permute-start(bf16[4,24,384]{2,1,0:T(8,128)(2,1)} %get-tuple-element.47), channel_id=1, source_target_pairs={{0,1},{1,2},{2,3},{4,5},{5,6},{6,7},{8,9},{9,10},{10,11},{12,13},{... | collective-permute-start | bytes 221192 | tf_op jit(solution)/shard_map/ppermute | solution.py:398
  8.0 4.2 %collective-permute-done.1.bot_ref = bf16[4,24,384]{2,1,0:T(8,128)(2,1)S(1)} collective-permute-done((bf16[4,24,384]{2,1,0:T(8,128)(2,1)}, bf16[4,24,384]{2,1,0:T(8,128)(2,1)S(1)}, u32[]{:S(2)}, u32[]{:S(2)}) %collective-permute-start.1) | collective-permute-done | bytes 73760 | tf_op jit(solution)/shard_map/ppermute | solution.py:399
  15.0 2.6 %collective-permute-start.5 = (bf16[4,192,384]{2,1,0:T(8,128)(2,1)}, bf16[4,192,384]{2,1,0:T(8,128)(2,1)S(1)}, u32[]{:S(2)}, u32[]{:S(2)}) collective-permute-start(bf16[4,192,384]{2,1,0:T(8,128)(2,1)} %bitcast.12), channel_id=1, source_target_pairs={{0,3},{1,0},{2,1},{3,2},{4,7},{5,4},{6,5},{7,6},{8,11},{9,8},{10,9... | collective-permute-start | bytes 1769480 | tf_op jit(solution)/shard_map/ppermute | solution.py:382
  17.6 1.9 %ends.1 = bf16[2,240,384]{2,1,0:T(8,128)(2,1)} custom-call(bf16[4,192,384]{2,1,0:T(8,128)(2,1)} %bitcast.13, bf16[4,24,384]{2,1,0:T(8,128)(2,1)} %copy-done.13, bf16[4,24,384]{2,1,0:T(8,128)(2,1)} %copy-done.14), custom_call_target="tpu_custom_call" | custom-call | tf_op jit(solution)/shard_map/ends/pallas_call | solution.py:403
  19.5 1.9 %collective-permute-start.2 = (bf16[2,240,384]{2,1,0:T(8,128)(2,1)}, bf16[2,240,384]{2,1,0:T(8,128)(2,1)S(1)}, u32[]{:S(2)}, u32[]{:S(2)}) collective-permute-start(bf16[2,240,384]{2,1,0:T(8,128)(2,1)} %ends.1), channel_id=1, source_target_pairs={{0,4},{4,8},{8,12},{12,16},{16,20},{20,24},{24,28},{28,32},{32,36}... | collective-permute-start | bytes 1105928 | tf_op jit(solution)/shard_map/ppermute | solution.py:404
  21.4 7.1 %collective-permute-done.2.ends_ref = bf16[2,240,384]{2,1,0:T(8,128)(2,1)S(1)} collective-permute-done((bf16[2,240,384]{2,1,0:T(8,128)(2,1)}, bf16[2,240,384]{2,1,0:T(8,128)(2,1)S(1)}, u32[]{:S(2)}, u32[]{:S(2)}) %collective-permute-start.2) | collective-permute-done | bytes 368672 | tf_op jit(solution)/shard_map/ppermute | solution.py:404
  29.3 14.5 %forward.1 = (f32[768,32]{1,0:T(8,128)}, bf16[128,768]{1,0:T(8,128)(2,1)}, bf16[128,768]{1,0:T(8,128)(2,1)}, bf16[128,768]{1,0:T(8,128)(2,1)}, bf16[128,768]{1,0:T(8,128)(2,1)}) custom-call(s32[21]{0:T(128)} %len_ref.3, bf16[4,192,384]{2,1,0:T(8,128)(2,1)} %bitcast.14, bf16[2,240,384]{2,1,0:T(8,128)(2,1)} %copy-done.12, bf16[4,24,384]{2,1,0:T(8,128)(2,1)} %copy-done.13, ...), custom_call_target="tpu_custom_call" | custom-call | tf_op jit(solution)/shard_map/forward/pallas_call | solution.py:411
  43.9 1.7 %collective-permute-start.7 = (bf16[128,768]{1,0:T(8,128)(2,1)}, bf16[128,768]{1,0:T(8,128)(2,1)S(1)}, u32[]{:S(2)}, u32[]{:S(2)}) collective-permute-start(bf16[128,768]{1,0:T(8,128)(2,1)} %get-tuple-element.59), channel_id=1, source_target_pairs={{0,2},{1,3},{2,0},{3,1},{4,6},{5,7},{6,4},{7,5},{8,10},{9,11},{10,... | collective-permute-start | bytes 589832 | tf_op jit(solution)/shard_map/ppermute | solution.py:382
  45.6 1.7 %collective-permute-start.8 = (bf16[128,768]{1,0:T(8,128)(2,1)}, bf16[128,768]{1,0:T(8,128)(2,1)S(1)}, u32[]{:S(2)}, u32[]{:S(2)}) collective-permute-start(bf16[128,768]{1,0:T(8,128)(2,1)} %get-tuple-element.60), channel_id=1, source_target_pairs={{0,3},{1,0},{2,1},{3,2},{4,7},{5,4},{6,5},{7,6},{8,11},{9,8},{10,9... | collective-permute-start | bytes 589832 | tf_op jit(solution)/shard_map/ppermute | solution.py:382
  47.4 5.6 %choose.1 = (bf16[4,768,256]{2,1,0:T(8,128)(2,1)}, bf16[4,768,256]{2,1,0:T(8,128)(2,1)}) custom-call(bf16[4,192,384]{2,1,0:T(8,128)(2,1)} %bitcast.15, bf16[4,192,384]{2,1,0:T(8,128)(2,1)} %copy-done.9, bf16[4,192,384]{2,1,0:T(8,128)(2,1)} %copy-done.10, bf16[4,192,384]{2,1,0:T(8,128)(2,1)} %copy-done.11, bf16[2,384,512]{2,1,0:T(8,128)(2,1)} %constant.2.clone.table_ref), custom_call_target="tpu_custom_call" | custom-call | tf_op jit(solution)/shard_map/choose/pallas_call | solution.py:433
  53.0 3.0 %collective-permute-done.6.refs_1_.a1 = bf16[128,768]{1,0:T(8,128)(2,1)S(1)} collective-permute-done((bf16[128,768]{1,0:T(8,128)(2,1)}, bf16[128,768]{1,0:T(8,128)(2,1)S(1)}, u32[]{:S(2)}, u32[]{:S(2)}) %collective-permute-start.6) | collective-permute-done | bytes 196640 | tf_op jit(solution)/shard_map/ppermute | solution.py:382
  57.7 2.3 %collective-permute-done.10.refs_5_.b1 = bf16[128,768]{1,0:T(8,128)(2,1)S(1)} collective-permute-done((bf16[128,768]{1,0:T(8,128)(2,1)S(1)}, bf16[128,768]{1,0:T(8,128)(2,1)S(1)}, u32[]{:S(2)}, u32[]{:S(2)}) %collective-permute-start.10) | collective-permute-done | bytes 196640 | tf_op jit(solution)/shard_map/ppermute | solution.py:376
  61.9 2.0 %clip.1 = (f32[8,128]{1,0:T(8,128)}, bf16[4,96,384]{2,1,0:T(8,128)(2,1)}) custom-call(bf16[128,768]{1,0:T(8,128)(2,1)} %get-tuple-element.66.refs_0_.a0, bf16[128,768]{1,0:T(8,128)(2,1)} %copy-done.2, bf16[128,768]{1,0:T(8,128)(2,1)} %copy-done.3, bf16[128,768]{1,0:T(8,128)(2,1)} %copy-done.4, bf16[128,768]{1,0:T(8,128)(2,1)} %copy-done.8, ...), custom_call_target="tpu_custom_call" | custom-call | tf_op jit(solution)/shard_map/clip/pallas_call | solution.py:447
  63.8 1.9 %collective-permute-start.13 = (f32[8,128]{1,0:T(8,128)}, f32[8,128]{1,0:T(8,128)S(1)}, u32[]{:S(2)}, u32[]{:S(2)}) collective-permute-start(f32[8,128]{1,0:T(8,128)} %get-tuple-element.71.mid_ref), channel_id=1, source_target_pairs={{0,8},{4,12},{8,16},{12,20},{16,24},{20,28},{24,32},{28,36},{32,40... | collective-permute-start | bytes 12296 | tf_op jit(solution)/shard_map/ppermute | solution.py:379
  65.9 1.8 %collective-permute-done.13 = f32[8,128]{1,0:T(8,128)S(1)} collective-permute-done((f32[8,128]{1,0:T(8,128)}, f32[8,128]{1,0:T(8,128)S(1)}, u32[]{:S(2)}, u32[]{:S(2)}) %collective-permute-start.13) | collective-permute-done | bytes 4128 | tf_op jit(solution)/shard_map/ppermute | solution.py:379
  67.7 3.1 %collective-permute-done.14 = f32[8,128]{1,0:T(8,128)S(1)} collective-permute-done((f32[8,128]{1,0:T(8,128)}, f32[8,128]{1,0:T(8,128)S(1)}, u32[]{:S(2)}, u32[]{:S(2)}) %collective-permute-start.14) | collective-permute-done | bytes 4128 | tf_op jit(solution)/shard_map/ppermute | solution.py:379
  73.0 2.1 %collective-permute-start.15 = (f32[3,8,128]{2,1,0:T(8,128)S(1)}, f32[3,8,128]{2,1,0:T(8,128)S(1)}, u32[]{:S(2)}, u32[]{:S(2)}) collective-permute-start(f32[3,8,128]{2,1,0:T(8,128)S(1)} %pad_maximum_fusion), channel_id=1, source_target_pairs={{0,16},{4,20},{8,24},{12,28},{16,32},{20,36},{24,40},{28,44},{32,4... | collective-permute-start | bytes 36872 | tf_op jit(solution)/shard_map/ppermute | solution.py:379
  75.1 4.1 %collective-permute-start.16 = (f32[3,8,128]{2,1,0:T(8,128)S(1)}, f32[3,8,128]{2,1,0:T(8,128)S(1)}, u32[]{:S(2)}, u32[]{:S(2)}) collective-permute-start(f32[3,8,128]{2,1,0:T(8,128)S(1)} %pad_maximum_fusion), channel_id=1, source_target_pairs={{0,240},{4,244},{8,248},{12,252},{16,0},{20,4},{24,8},{28,12},{32,... | collective-permute-start | bytes 36872 | tf_op jit(solution)/shard_map/ppermute | solution.py:379
  79.3 1.7 %collective-permute-done.15.left_ref = f32[3,8,128]{2,1,0:T(8,128)S(1)} collective-permute-done((f32[3,8,128]{2,1,0:T(8,128)S(1)}, f32[3,8,128]{2,1,0:T(8,128)S(1)}, u32[]{:S(2)}, u32[]{:S(2)}) %collective-permute-start.15) | collective-permute-done | bytes 12320 | tf_op jit(solution)/shard_map/ppermute | solution.py:379
  82.3 15.6 %weight.1 = (f32[3,48,896]{2,1,0:T(8,128)}, bf16[3,48,896]{2,1,0:T(8,128)(2,1)}, bf16[3,48,896]{2,1,0:T(8,128)(2,1)}, bf16[3,48,896]{2,1,0:T(8,128)(2,1)}) custom-call(s32[21]{0:T(128)} %len_ref.3, f32[3,8,128]{2,1,0:T(8,128)} %copy-done.23, f32[8,128]{1,0:T(8,128)} %get-tuple-element.71.mid_ref, f32[3,8,128]{2,1,0:T(8,128)} %copy-done.24, ...), custom_call_target="tpu_custom_call" | custom-call | tf_op jit(solution)/shard_map/weight/pallas_call | solution.py:463
  99.6 2.9 %collective-permute-start.20 = (bf16[3,48,896]{2,1,0:T(8,128)(2,1)}, bf16[3,48,896]{2,1,0:T(8,128)(2,1)S(1)}, u32[]{:S(2)}, u32[]{:S(2)}) collective-permute-start(bf16[3,48,896]{2,1,0:T(8,128)(2,1)} %get-tuple-element.79), channel_id=1, source_target_pairs={{0,128},{4,132},{8,136},{12,140},{16,144},{20,148},{24,152},{28,15... | collective-permute-start | bytes 774152 | tf_op jit(solution)/shard_map/ppermute | solution.py:385
  103.8 4.0 %collective-permute-done.19.refs_1_ = bf16[3,48,896]{2,1,0:T(8,128)(2,1)S(1)} collective-permute-done((bf16[3,48,896]{2,1,0:T(8,128)(2,1)}, bf16[3,48,896]{2,1,0:T(8,128)(2,1)S(1)}, u32[]{:S(2)}, u32[]{:S(2)}) %collective-permute-start.19) | collective-permute-done | bytes 258080 | tf_op jit(solution)/shard_map/ppermute | solution.py:385
  107.8 4.5 %collective-permute-done.20.refs_2_ = bf16[3,48,896]{2,1,0:T(8,128)(2,1)S(1)} collective-permute-done((bf16[3,48,896]{2,1,0:T(8,128)(2,1)}, bf16[3,48,896]{2,1,0:T(8,128)(2,1)S(1)}, u32[]{:S(2)}, u32[]{:S(2)}) %collective-permute-start.20) | collective-permute-done | bytes 258080 | tf_op jit(solution)/shard_map/ppermute | solution.py:385
  113.1 2.5 %add.1 = (f32[4,24,896]{2,1,0:T(8,128)}, bf16[4,24,896]{2,1,0:T(8,128)(2,1)}) custom-call(f32[3,48,896]{2,1,0:T(8,128)} %get-tuple-element.77.refs_0_, bf16[3,48,896]{2,1,0:T(8,128)(2,1)} %copy-done.16, bf16[3,48,896]{2,1,0:T(8,128)(2,1)} %copy-done.17, bf16[3,48,896]{2,1,0:T(8,128)(2,1)} %copy-done.18), custom_call_target="tpu_custom_call" | custom-call | tf_op jit(solution)/shard_map/add/pallas_call | solution.py:483
  115.6 4.3 %collective-permute-start.22 = (bf16[4,24,896]{2,1,0:T(8,128)(2,1)}, bf16[4,24,896]{2,1,0:T(8,128)(2,1)S(1)}, u32[]{:S(2)}, u32[]{:S(2)}) collective-permute-start(bf16[4,24,896]{2,1,0:T(8,128)(2,1)} %get-tuple-element.82), channel_id=1, source_target_pairs={{0,8},{4,12},{8,0},{12,4},{16,24},{20,28},{24,16},{28,20},{32,40},... | collective-permute-start | bytes 516104 | tf_op jit(solution)/shard_map/ppermute | solution.py:489
  119.9 3.6 %collective-permute-done.22.got_ref = bf16[4,24,896]{2,1,0:T(8,128)(2,1)S(1)} collective-permute-done((bf16[4,24,896]{2,1,0:T(8,128)(2,1)}, bf16[4,24,896]{2,1,0:T(8,128)(2,1)S(1)}, u32[]{:S(2)}, u32[]{:S(2)}) %collective-permute-start.22) | collective-permute-done | bytes 172064 | tf_op jit(solution)/shard_map/ppermute | solution.py:489
  124.2 1.7 %pair.1 = (f32[24,896]{1,0:T(8,128)}, bf16[24,896]{1,0:T(8,128)(2,1)}, bf16[24,896]{1,0:T(8,128)(2,1)}, bf16[24,896]{1,0:T(8,128)(2,1)}) custom-call(f32[4,24,896]{2,1,0:T(8,128)} %get-tuple-element.81.keep_ref, bf16[4,24,896]{2,1,0:T(8,128)(2,1)} %copy-done.19), custom_call_target="tpu_custom_call" | custom-call | tf_op jit(solution)/shard_map/pair/pallas_call | solution.py:490
  126.5 6.3 %collective-permute-start.24 = (bf16[24,896]{1,0:T(8,128)(2,1)}, bf16[24,896]{1,0:T(8,128)(2,1)S(1)}, u32[]{:S(2)}, u32[]{:S(2)}) collective-permute-start(bf16[24,896]{1,0:T(8,128)(2,1)} %get-tuple-element.85), channel_id=1, source_target_pairs={{0,32},{4,36},{8,40},{12,44},{16,48},{20,52},{24,56},{28,60},{32,0... | collective-permute-start | bytes 129032 | tf_op jit(solution)/shard_map/ppermute | solution.py:388
  132.9 2.5 %collective-permute-done.24.refs_2_ = bf16[24,896]{1,0:T(8,128)(2,1)S(1)} collective-permute-done((bf16[24,896]{1,0:T(8,128)(2,1)}, bf16[24,896]{1,0:T(8,128)(2,1)S(1)}, u32[]{:S(2)}, u32[]{:S(2)}) %collective-permute-start.24) | collective-permute-done | bytes 43040 | tf_op jit(solution)/shard_map/ppermute | solution.py:388
  135.4 2.5 %collective-permute-done.25.refs_3_ = bf16[24,896]{1,0:T(8,128)(2,1)S(1)} collective-permute-done((bf16[24,896]{1,0:T(8,128)(2,1)}, bf16[24,896]{1,0:T(8,128)(2,1)S(1)}, u32[]{:S(2)}, u32[]{:S(2)}) %collective-permute-start.25) | collective-permute-done | bytes 43040 | tf_op jit(solution)/shard_map/ppermute | solution.py:388
  138.5 1.8 %last.1 = (f32[6,27,96]{2,1,0:T(8,128)}, f32[6,8]{1,0:T(8,128)}, f32[1,1]{1,0:T(1,128)}) custom-call(f32[24,896]{1,0:T(8,128)} %get-tuple-element.83.refs_0_, bf16[24,896]{1,0:T(8,128)(2,1)} %copy-done.20, bf16[24,896]{1,0:T(8,128)(2,1)} %copy-done.21, bf16[24,896]{1,0:T(8,128)(2,1)} %copy-done.22), custom_call_target="tpu_custom_call" | custom-call | tf_op jit(solution)/shard_map/last/pallas_call | solution.py:497
  (80 shorter events, 19.0 us)
Async XLA Ops:
  2.4 5.7 %collective-permute-start = (bf16[4,24,384]{2,1,0:T(8,128)(2,1)}, bf16[4,24,384]{2,1,0:T(8,128)(2,1)S(1)}, u32[]{:S(2)}, u32[]{:S(2)}) collective-permute-start(bf16[4,24,384]{2,1,0:T(8,128)(2,1)} %get-tuple-element.47), channel_id=1, source_target_pairs={{0,1},{1,2},{2,3},{4,5},{5,6},{6,7},{8,9},{9,10},{10,11},{12,13},{... | collective-permute-start | bytes 221192 | tf_op jit(solution)/shard_map/ppermute | solution.py:398
  5.8 6.5 %collective-permute-start.1 = (bf16[4,24,384]{2,1,0:T(8,128)(2,1)}, bf16[4,24,384]{2,1,0:T(8,128)(2,1)S(1)}, u32[]{:S(2)}, u32[]{:S(2)}) collective-permute-start(bf16[4,24,384]{2,1,0:T(8,128)(2,1)} %get-tuple-element.48), channel_id=1, source_target_pairs={{1,0},{2,1},{3,2},{5,4},{6,5},{7,6},{9,8},{10,9},{11,10},{13,12},{... | collective-permute-start | bytes 221192 | tf_op jit(solution)/shard_map/ppermute | solution.py:399
  8.0 9.5 %copy-start.13 = (bf16[4,24,384]{2,1,0:T(8,128)(2,1)}, bf16[4,24,384]{2,1,0:T(8,128)(2,1)S(1)}, u32[]{:S(2)}) copy-start(bf16[4,24,384]{2,1,0:T(8,128)(2,1)S(1)} %collective-permute-done.top_ref) | copy-start | bytes 221188
  12.2 5.4 %copy-start.14 = (bf16[4,24,384]{2,1,0:T(8,128)(2,1)}, bf16[4,24,384]{2,1,0:T(8,128)(2,1)S(1)}, u32[]{:S(2)}) copy-start(bf16[4,24,384]{2,1,0:T(8,128)(2,1)S(1)} %collective-permute-done.1.bot_ref) | copy-start | bytes 221188
  12.2 31.6 %collective-permute-start.3 = (bf16[4,192,384]{2,1,0:T(8,128)(2,1)}, bf16[4,192,384]{2,1,0:T(8,128)(2,1)S(1)}, u32[]{:S(2)}, u32[]{:S(2)}) collective-permute-start(bf16[4,192,384]{2,1,0:T(8,128)(2,1)} %bitcast.10), channel_id=1, source_target_pairs={{0,1},{1,2},{2,3},{3,0},{4,5},{5,6},{6,7},{7,4},{8,9},{9,10},{10,1... | collective-permute-start | bytes 1769480 | tf_op jit(solution)/shard_map/ppermute | solution.py:382
  13.7 30.1 %collective-permute-start.4 = (bf16[4,192,384]{2,1,0:T(8,128)(2,1)}, bf16[4,192,384]{2,1,0:T(8,128)(2,1)S(1)}, u32[]{:S(2)}, u32[]{:S(2)}) collective-permute-start(bf16[4,192,384]{2,1,0:T(8,128)(2,1)} %bitcast.11), channel_id=1, source_target_pairs={{0,2},{1,3},{2,0},{3,1},{4,6},{5,7},{6,4},{7,5},{8,10},{9,11},{10,... | collective-permute-start | bytes 1769480 | tf_op jit(solution)/shard_map/ppermute | solution.py:382
  15.0 28.9 %collective-permute-start.5 = (bf16[4,192,384]{2,1,0:T(8,128)(2,1)}, bf16[4,192,384]{2,1,0:T(8,128)(2,1)S(1)}, u32[]{:S(2)}, u32[]{:S(2)}) collective-permute-start(bf16[4,192,384]{2,1,0:T(8,128)(2,1)} %bitcast.12), channel_id=1, source_target_pairs={{0,3},{1,0},{2,1},{3,2},{4,7},{5,4},{6,5},{7,6},{8,11},{9,8},{10,9... | collective-permute-start | bytes 1769480 | tf_op jit(solution)/shard_map/ppermute | solution.py:382
  19.5 9.0 %collective-permute-start.2 = (bf16[2,240,384]{2,1,0:T(8,128)(2,1)}, bf16[2,240,384]{2,1,0:T(8,128)(2,1)S(1)}, u32[]{:S(2)}, u32[]{:S(2)}) collective-permute-start(bf16[2,240,384]{2,1,0:T(8,128)(2,1)} %ends.1), channel_id=1, source_target_pairs={{0,4},{4,8},{8,12},{12,16},{16,20},{20,24},{24,28},{28,32},{32,36}... | collective-permute-start | bytes 1105928 | tf_op jit(solution)/shard_map/ppermute | solution.py:404
  43.8 13.8 %copy-start.1 = (bf16[128,768]{1,0:T(8,128)(2,1)S(1)}, bf16[128,768]{1,0:T(8,128)(2,1)}, u32[]{:S(2)}) copy-start(bf16[128,768]{1,0:T(8,128)(2,1)} %get-tuple-element.66.refs_0_.a0) | copy-start | bytes 589828
  43.8 12.2 %collective-permute-start.6 = (bf16[128,768]{1,0:T(8,128)(2,1)}, bf16[128,768]{1,0:T(8,128)(2,1)S(1)}, u32[]{:S(2)}, u32[]{:S(2)}) collective-permute-start(bf16[128,768]{1,0:T(8,128)(2,1)} %get-tuple-element.58), channel_id=1, source_target_pairs={{0,1},{1,2},{2,3},{3,0},{4,5},{5,6},{6,7},{7,4},{8,9},{9,10},{10,1... | collective-permute-start | bytes 589832 | tf_op jit(solution)/shard_map/ppermute | solution.py:382
  43.9 12.1 %collective-permute-start.7 = (bf16[128,768]{1,0:T(8,128)(2,1)}, bf16[128,768]{1,0:T(8,128)(2,1)S(1)}, u32[]{:S(2)}, u32[]{:S(2)}) collective-permute-start(bf16[128,768]{1,0:T(8,128)(2,1)} %get-tuple-element.59), channel_id=1, source_target_pairs={{0,2},{1,3},{2,0},{3,1},{4,6},{5,7},{6,4},{7,5},{8,10},{9,11},{10,... | collective-permute-start | bytes 589832 | tf_op jit(solution)/shard_map/ppermute | solution.py:382
  45.6 11.0 %collective-permute-start.8 = (bf16[128,768]{1,0:T(8,128)(2,1)}, bf16[128,768]{1,0:T(8,128)(2,1)S(1)}, u32[]{:S(2)}, u32[]{:S(2)}) collective-permute-start(bf16[128,768]{1,0:T(8,128)(2,1)} %get-tuple-element.60), channel_id=1, source_target_pairs={{0,3},{1,0},{2,1},{3,2},{4,7},{5,4},{6,5},{7,6},{8,11},{9,8},{10,9... | collective-permute-start | bytes 589832 | tf_op jit(solution)/shard_map/ppermute | solution.py:382
  56.0 4.8 %copy-start.2 = (bf16[128,768]{1,0:T(8,128)(2,1)}, bf16[128,768]{1,0:T(8,128)(2,1)S(1)}, u32[]{:S(2)}) copy-start(bf16[128,768]{1,0:T(8,128)(2,1)S(1)} %collective-permute-done.6.refs_1_.a1) | copy-start | bytes 589828
  56.0 4.8 %copy-start.3 = (bf16[128,768]{1,0:T(8,128)(2,1)}, bf16[128,768]{1,0:T(8,128)(2,1)S(1)}, u32[]{:S(2)}) copy-start(bf16[128,768]{1,0:T(8,128)(2,1)S(1)} %collective-permute-done.7.refs_2_.a2) | copy-start | bytes 589828
  56.6 24.4 %collective-permute-start.18 = (bf16[4,768,256]{2,1,0:T(8,128)(2,1)}, bf16[4,768,256]{2,1,0:T(8,128)(2,1)S(1)}, u32[]{:S(2)}, u32[]{:S(2)}) collective-permute-start(bf16[4,768,256]{2,1,0:T(8,128)(2,1)} %get-tuple-element.76), channel_id=1, source_target_pairs={{0,4},{4,0},{8,12},{12,8},{16,20},{20,16},{24,28},{28,24},{32,36},... | collective-permute-start | bytes 4718600 | tf_op jit(solution)/shard_map/ppermute | solution.py:376
  56.6 3.3 %collective-permute-start.10 = (bf16[128,768]{1,0:T(8,128)(2,1)S(1)}, bf16[128,768]{1,0:T(8,128)(2,1)S(1)}, u32[]{:S(2)}, u32[]{:S(2)}) collective-permute-start(bf16[128,768]{1,0:T(8,128)(2,1)S(1)} %collective-permute-done.6.refs_1_.a1), channel_id=1, source_target_pairs={{0,4},{4,0},{8,12},{12,8},{16,20},{20,16},{24,28},{28,24},{32,36},... | collective-permute-start | bytes 589832 | tf_op jit(solution)/shard_map/ppermute | solution.py:376
  57.1 3.1 %collective-permute-start.11 = (bf16[128,768]{1,0:T(8,128)(2,1)S(1)}, bf16[128,768]{1,0:T(8,128)(2,1)S(1)}, u32[]{:S(2)}, u32[]{:S(2)}) collective-permute-start(bf16[128,768]{1,0:T(8,128)(2,1)S(1)} %collective-permute-done.7.refs_2_.a2), channel_id=1, source_target_pairs={{0,4},{4,0},{8,12},{12,8},{16,20},{20,16},{24,28},{28,24},{32,36},... | collective-permute-start | bytes 589832 | tf_op jit(solution)/shard_map/ppermute | solution.py:376
  57.1 3.4 %collective-permute-start.12 = (bf16[128,768]{1,0:T(8,128)(2,1)S(1)}, bf16[128,768]{1,0:T(8,128)(2,1)S(1)}, u32[]{:S(2)}, u32[]{:S(2)}) collective-permute-start(bf16[128,768]{1,0:T(8,128)(2,1)S(1)} %collective-permute-done.8.refs_3_.a3), channel_id=1, source_target_pairs={{0,4},{4,0},{8,12},{12,8},{16,20},{20,16},{24,28},{28,24},{32,36},... | collective-permute-start | bytes 589832 | tf_op jit(solution)/shard_map/ppermute | solution.py:376
  57.7 3.1 %collective-permute-start.9 = (bf16[128,768]{1,0:T(8,128)(2,1)S(1)}, bf16[128,768]{1,0:T(8,128)(2,1)S(1)}, u32[]{:S(2)}, u32[]{:S(2)}) collective-permute-start(bf16[128,768]{1,0:T(8,128)(2,1)S(1)} %copy-done.1), channel_id=1, source_target_pairs={{0,4},{4,0},{8,12},{12,8},{16,20},{20,16},{24,28},{28,24},{32,36},... | collective-permute-start | bytes 589832 | tf_op jit(solution)/shard_map/ppermute | solution.py:376
  63.8 3.8 %collective-permute-start.13 = (f32[8,128]{1,0:T(8,128)}, f32[8,128]{1,0:T(8,128)S(1)}, u32[]{:S(2)}, u32[]{:S(2)}) collective-permute-start(f32[8,128]{1,0:T(8,128)} %get-tuple-element.71.mid_ref), channel_id=1, source_target_pairs={{0,8},{4,12},{8,16},{12,20},{16,24},{20,28},{24,32},{28,36},{32,40... | collective-permute-start | bytes 12296 | tf_op jit(solution)/shard_map/ppermute | solution.py:379
  65.8 5.0 %collective-permute-start.14 = (f32[8,128]{1,0:T(8,128)}, f32[8,128]{1,0:T(8,128)S(1)}, u32[]{:S(2)}, u32[]{:S(2)}) collective-permute-start(f32[8,128]{1,0:T(8,128)} %get-tuple-element.71.mid_ref), channel_id=1, source_target_pairs={{0,248},{4,252},{8,0},{12,4},{16,8},{20,12},{24,16},{28,20},{32,24... | collective-permute-start | bytes 12296 | tf_op jit(solution)/shard_map/ppermute | solution.py:379
  70.7 10.3 %collective-permute-start.17 = (bf16[4,96,384]{2,1,0:T(8,128)(2,1)}, bf16[4,96,384]{2,1,0:T(8,128)(2,1)S(1)}, u32[]{:S(2)}, u32[]{:S(2)}) collective-permute-start(bf16[4,96,384]{2,1,0:T(8,128)(2,1)} %get-tuple-element.74), channel_id=1, source_target_pairs={{0,248},{4,252},{8,0},{12,4},{16,8},{20,12},{24,16},{28,20},{32,24... | collective-permute-start | bytes 884744 | tf_op jit(solution)/shard_map/ppermute | solution.py:379
  73.0 7.9 %collective-permute-start.15 = (f32[3,8,128]{2,1,0:T(8,128)S(1)}, f32[3,8,128]{2,1,0:T(8,128)S(1)}, u32[]{:S(2)}, u32[]{:S(2)}) collective-permute-start(f32[3,8,128]{2,1,0:T(8,128)S(1)} %pad_maximum_fusion), channel_id=1, source_target_pairs={{0,16},{4,20},{8,24},{12,28},{16,32},{20,36},{24,40},{28,44},{32,4... | collective-permute-start | bytes 36872 | tf_op jit(solution)/shard_map/ppermute | solution.py:379
  75.1 5.9 %collective-permute-start.16 = (f32[3,8,128]{2,1,0:T(8,128)S(1)}, f32[3,8,128]{2,1,0:T(8,128)S(1)}, u32[]{:S(2)}, u32[]{:S(2)}) collective-permute-start(f32[3,8,128]{2,1,0:T(8,128)S(1)} %pad_maximum_fusion), channel_id=1, source_target_pairs={{0,240},{4,244},{8,248},{12,252},{16,0},{20,4},{24,8},{28,12},{32,... | collective-permute-start | bytes 36872 | tf_op jit(solution)/shard_map/ppermute | solution.py:379
  97.9 9.9 %collective-permute-start.19 = (bf16[3,48,896]{2,1,0:T(8,128)(2,1)}, bf16[3,48,896]{2,1,0:T(8,128)(2,1)S(1)}, u32[]{:S(2)}, u32[]{:S(2)}) collective-permute-start(bf16[3,48,896]{2,1,0:T(8,128)(2,1)} %get-tuple-element.78), channel_id=1, source_target_pairs={{0,64},{4,68},{8,72},{12,76},{16,80},{20,84},{24,88},{28,92},{32,9... | collective-permute-start | bytes 774152 | tf_op jit(solution)/shard_map/ppermute | solution.py:385
  99.6 12.7 %collective-permute-start.20 = (bf16[3,48,896]{2,1,0:T(8,128)(2,1)}, bf16[3,48,896]{2,1,0:T(8,128)(2,1)S(1)}, u32[]{:S(2)}, u32[]{:S(2)}) collective-permute-start(bf16[3,48,896]{2,1,0:T(8,128)(2,1)} %get-tuple-element.79), channel_id=1, source_target_pairs={{0,128},{4,132},{8,136},{12,140},{16,144},{20,148},{24,152},{28,15... | collective-permute-start | bytes 774152 | tf_op jit(solution)/shard_map/ppermute | solution.py:385
  102.5 9.8 %collective-permute-start.21 = (bf16[3,48,896]{2,1,0:T(8,128)(2,1)}, bf16[3,48,896]{2,1,0:T(8,128)(2,1)S(1)}, u32[]{:S(2)}, u32[]{:S(2)}) collective-permute-start(bf16[3,48,896]{2,1,0:T(8,128)(2,1)} %get-tuple-element.80), channel_id=1, source_target_pairs={{0,192},{4,196},{8,200},{12,204},{16,208},{20,212},{24,216},{28,22... | collective-permute-start | bytes 774152 | tf_op jit(solution)/shard_map/ppermute | solution.py:385
  115.6 7.9 %collective-permute-start.22 = (bf16[4,24,896]{2,1,0:T(8,128)(2,1)}, bf16[4,24,896]{2,1,0:T(8,128)(2,1)S(1)}, u32[]{:S(2)}, u32[]{:S(2)}) collective-permute-start(bf16[4,24,896]{2,1,0:T(8,128)(2,1)} %get-tuple-element.82), channel_id=1, source_target_pairs={{0,8},{4,12},{8,0},{12,4},{16,24},{20,28},{24,16},{28,20},{32,40},... | collective-permute-start | bytes 516104 | tf_op jit(solution)/shard_map/ppermute | solution.py:489
  125.9 7.0 %collective-permute-start.23 = (bf16[24,896]{1,0:T(8,128)(2,1)}, bf16[24,896]{1,0:T(8,128)(2,1)S(1)}, u32[]{:S(2)}, u32[]{:S(2)}) collective-permute-start(bf16[24,896]{1,0:T(8,128)(2,1)} %get-tuple-element.84), channel_id=1, source_target_pairs={{0,16},{4,20},{8,24},{12,28},{16,32},{20,36},{24,40},{28,44},{32,4... | collective-permute-start | bytes 129032 | tf_op jit(solution)/shard_map/ppermute | solution.py:388
  126.5 8.9 %collective-permute-start.24 = (bf16[24,896]{1,0:T(8,128)(2,1)}, bf16[24,896]{1,0:T(8,128)(2,1)S(1)}, u32[]{:S(2)}, u32[]{:S(2)}) collective-permute-start(bf16[24,896]{1,0:T(8,128)(2,1)} %get-tuple-element.85), channel_id=1, source_target_pairs={{0,32},{4,36},{8,40},{12,44},{16,48},{20,52},{24,56},{28,60},{32,0... | collective-permute-start | bytes 129032 | tf_op jit(solution)/shard_map/ppermute | solution.py:388
  132.7 5.1 %collective-permute-start.25 = (bf16[24,896]{1,0:T(8,128)(2,1)}, bf16[24,896]{1,0:T(8,128)(2,1)S(1)}, u32[]{:S(2)}, u32[]{:S(2)}) collective-permute-start(bf16[24,896]{1,0:T(8,128)(2,1)} %get-tuple-element.86), channel_id=1, source_target_pairs={{0,48},{4,52},{8,56},{12,60},{16,0},{20,4},{24,8},{28,12},{32,16},... | collective-permute-start | bytes 129032 | tf_op jit(solution)/shard_map/ppermute | solution.py:388
  132.9 4.9 %copy-start.20 = (bf16[24,896]{1,0:T(8,128)(2,1)}, bf16[24,896]{1,0:T(8,128)(2,1)S(1)}, u32[]{:S(2)}) copy-start(bf16[24,896]{1,0:T(8,128)(2,1)S(1)} %collective-permute-done.23.refs_1_) | copy-start | bytes 129028
  (19 other events, 31.4 us)

commit v2 on v1

--- a/solution.py
+++ b/solution.py
@@ -174,25 +174,29 @@
         ref[16:32] = both.astype(B16)
 
 
+def tail_kernel(a0, a1, a2, a3, out_ref):
+    x = lax.axis_index("space")
+    for d, ref in enumerate((a0, a1, a2, a3)):
+        out_ref[lax.rem(x - d + 4, 4)] = ref[32:, :]
+
+
 def clip_kernel(*refs):
-    c, x = lax.rem(lax.axis_index("tm"), 2), lax.axis_index("space")
-    given, (sums_ref, tail_ref) = (refs[:4], refs[4:8]), refs[8:]
+    c = lax.rem(lax.axis_index("tm"), 2)
+    given, sums_ref = (refs[:4], refs[4:8]), refs[8]
     sums = []
     for four in given:
-        v = four[0][:16, :128].astype(F32)
+        v = four[0][...].astype(F32)
         for ref in four[1:]:
-            v = v + ref[:16, :128].astype(F32)
+            v = v + ref[...].astype(F32)
         sums.append(v[:4] + v[4:8] + v[8:12])
     for core in range(2):
 
         @pl.when(c == core)
         def _():
             sums_ref[...] = jnp.concatenate([sums[core], sums[1 - core]], axis=0)
-            for d in range(4):
-                tail_ref[lax.rem(x - d + 4, 4)] = given[core][d][32:, :]
-
-
-def weight_kernel(ny, nz, per_frame, len_ref, left_ref, mid_ref, right_ref, next_ref, a0, a1, a2, a3, b0, b1, b2, b3,
+
+
+def weight_kernel(ny, nz, per_frame, len_ref, left_ref, mid_ref, right_ref, next_ref, more_ref, a0, a1, a2, a3, b0, b1, b2, b3,
                   x_ref, xo_ref, table_ref, *refs):
     sends, (held_ref, taps_ref, acc_ref, out_ref, xs_ref, g_ref, keep_ref, sem) = refs[:ny], refs[ny:]
     c, x, y, _, k = place(nz)
@@ -257,7 +261,7 @@
             if f < 8:
                 v = held_ref[core, xs, 32:, :].astype(F32)
             else:
-                v = next_ref[xs].astype(F32)
+                v = next_ref[xs].astype(F32) + more_ref[xs].astype(F32)
                 v = jnp.concatenate([v, jnp.zeros_like(v)], axis=1)
             shift = ((xs - lf) * band) % full
             if shift:
@@ -444,17 +448,27 @@
     xoth = over_core(xoth)
 
     front = pl.BlockSpec((message.shape[0], 2 * band), lambda i: (0, 0))
-    kchip, tail = call(
+    tail = call(
+        tail_kernel,
+        shape((4, block, 2 * band), B16),
+        grid=(1,),
+        in_specs=[front] * 4,
+        out_specs=whole(4, block, 2 * band),
+        name="tail",
+    )(*mine_d)
+    tail = lax.ppermute(tail, "tm", [(i, i - 2) for i in range(2, count, 2)])
+    tail, core_d = lax.optimization_barrier((tail, core_d))
+    other = lax.ppermute(tail, "tm", [(i, i + 1) for i in range(0, count, 2)])
+    corner = pl.BlockSpec((16, 128), lambda i: (0, 0))
+    kchip = call(
         clip_kernel,
-        [shape((chip, 128), F32), shape((4, block, 2 * band), B16)],
+        shape((chip, 128), F32),
         grid=(1,),
-        in_specs=[front] * 8,
-        out_specs=[whole(chip, 128), whole(4, block, 2 * band)],
+        in_specs=[corner] * 8,
+        out_specs=whole(chip, 128),
         name="clip",
     )(*mine_d, *core_d)
     before, after = over_chip(kchip, 1), over_chip(kchip, -1)
-    tail, before, after = lax.optimization_barrier((tail, before, after))
-    tail = over_chip(tail, -1)
     triple = jnp.stack([before, kchip, after])
     left, right = over_chip(triple, 2), over_chip(triple, -2)
 
@@ -473,9 +487,9 @@
             pltpu.VMEM((3, 2 * chip, 128), F32),
             pltpu.SemaphoreType.DMA((3, 4)),
         ],
-        in_specs=[smem()] + [vmem()] * 4 + [pl.BlockSpec(memory_space=pl.ANY)] * 10 + [vmem()],
+        in_specs=[smem()] + [vmem()] * 5 + [pl.BlockSpec(memory_space=pl.ANY)] * 10 + [vmem()],
         name="weight",
-    )(clip_len, left, kchip, right, tail, *mine_d, *core_d, xown, xoth, table)
+    )(clip_len, left, kchip, right, tail, other, *mine_d, *core_d, xown, xoth, table)
     gets = [sends[0]] + [over_y(sends[d], d) for d in range(1, ny)]
     step = wide(run)
     chunk = 128 if wrow % 128 == 0 else wrow

time: 142 us -> 143 us (level)
  waiting for transfers between devices: 42.8 us -> 46.1 us
    ppermute x0 -> x2, waiting for transfers between devices: none -> 4.6 us  [the longest x1 4.59 us: body(): tail = lax.ppermute(tail, 'tm', [(i, i - 2) for i in range(2, count, 2)])]
    ppermute x1, starting transfers between devices: 4.33 us -> 0.6 us  [body(): lax.ppermute(sent, 'tm', [(index(a, b, e), index(a, b ^ 1, e)) for a, b,...]
    ppermute x0 -> x2, starting transfers between devices: none -> 3.2 us  [the longest x1 1.91 us: body(): tail = lax.ppermute(tail, 'tm', [(i, i - 2) for i in range(2, count, 2)])]
    ppermute x1, waiting for transfers between devices: 3.59 us -> 5.94 us  [body(): lax.ppermute(sent, 'tm', [(index(a, b, e), index(a, b ^ 1, e)) for a, b,...]
    ppermute x3, waiting for transfers between devices: 8.47 us -> 6.23 us  [over_y(): lax.ppermute(v, 'tm', [(index(a, b, e), index(a + d, b, e)) for a, b, e i...]
    ppermute x5, waiting for transfers between devices: 3.13 us -> 1.6 us  [over_core(): return lax.ppermute(v, 'tm', [(i, i ^ 1) for i in range(count)])]
    pallas_call x1 -> x2, Pallas kernels: 1.96 us -> 3.1 us  [the longest x1 1.76 us: body(): call(tail_kernel, shape((4, block, 2 * band), B16), grid=(1,), in_specs=[...]
    unnamed x50 -> x52, local copies, waits for them, and re-layouts: 5.21 us -> 4.19 us
  transfers between devices with their start and end apart: 26 -> 27, of which waited for: 19 -> 18; matrix products, arithmetic and copies ran while one was open for 0% -> 0% of each run, Pallas kernels for 17% -> 18%
where the time goes in v2:
time: 143 us
  Pallas kernels  48.6 us (34%)
  waiting for transfers between devices  46.1 us (32%)
  starting transfers between devices  42.1 us (29%)
  local copies, waits for them, and re-layouts  4.19 us (3%)
    pallas_call x1, Pallas kernels, body(): call(functools.partial(weight_kernel, ny, nz, float(4 * band)), [shape((3...  15.7 us
    pallas_call x1, Pallas kernels, body(): call(forward_kernel, [shape((cells, zlat), F32)] + [message] * 4, [pltpu....  14.5 us
    ppermute x4, starting transfers between devices, over_chip(): lax.ppermute(v, 'tm', [(i, (i + 2 * d) % count) for i in range(count)])  9.27 us
    ppermute x6, starting transfers between devices, over_x(): return lax.ppermute(v, 'space', [(i, (i + d) % 4) for i in range(4)])  8.86 us
    ppermute x1, waiting for transfers between devices, body(): ends = lax.ppermute(ends, 'tm', [(i, i + 1) for i in range(count - 1)])  7.11 us
    ppermute x3, starting transfers between devices, over_z(): lax.ppermute(v, 'tm', [(index(a, b, e), index(a, b + d, e)) for a, b, e i...  6.9 us
    ppermute x4, waiting for transfers between devices, over_chip(): lax.ppermute(v, 'tm', [(i, (i + 2 * d) % count) for i in range(count)])  6.72 us
    ppermute x3, waiting for transfers between devices, over_y(): lax.ppermute(v, 'tm', [(index(a, b, e), index(a + d, b, e)) for a, b, e i...  6.23 us
  transfers between devices with their start and end apart: 27, of which 18 were waited for; matrix products, arithmetic and copies ran while one was open for 0% of the time, Pallas kernels for 18%

profile of v2, /device:TPU:32, one launch (start us, length us, event | category | flops | bytes accessed | tf_op | source)
XLA Modules:
  0.0 142.6 jit_solution(1784716349859327278)
XLA Ops:
  0.6 1.7 %first.1 = (bf16[4,24,384]{2,1,0:T(8,128)(2,1)}, bf16[4,24,384]{2,1,0:T(8,128)(2,1)}) custom-call(bf16[4,192,384]{2,1,0:T(8,128)(2,1)} %bitcast.9), custom_call_target="tpu_custom_call" | custom-call | tf_op jit(solution)/shard_map/first/pallas_call | solution.py:400
  2.4 3.4 %collective-permute-start = (bf16[4,24,384]{2,1,0:T(8,128)(2,1)}, bf16[4,24,384]{2,1,0:T(8,128)(2,1)S(1)}, u32[]{:S(2)}, u32[]{:S(2)}) collective-permute-start(bf16[4,24,384]{2,1,0:T(8,128)(2,1)} %get-tuple-element.47), channel_id=1, source_target_pairs={{0,1},{1,2},{2,3},{4,5},{5,6},{6,7},{8,9},{9,10},{10,11},{12,13},{... | collective-permute-start | bytes 221192 | tf_op jit(solution)/shard_map/ppermute | solution.py:402
  8.0 4.2 %collective-permute-done.1.bot_ref = bf16[4,24,384]{2,1,0:T(8,128)(2,1)S(1)} collective-permute-done((bf16[4,24,384]{2,1,0:T(8,128)(2,1)}, bf16[4,24,384]{2,1,0:T(8,128)(2,1)S(1)}, u32[]{:S(2)}, u32[]{:S(2)}) %collective-permute-start.1) | collective-permute-done | bytes 73760 | tf_op jit(solution)/shard_map/ppermute | solution.py:403
  15.0 2.6 %collective-permute-start.5 = (bf16[4,192,384]{2,1,0:T(8,128)(2,1)}, bf16[4,192,384]{2,1,0:T(8,128)(2,1)S(1)}, u32[]{:S(2)}, u32[]{:S(2)}) collective-permute-start(bf16[4,192,384]{2,1,0:T(8,128)(2,1)} %bitcast.12), channel_id=1, source_target_pairs={{0,3},{1,0},{2,1},{3,2},{4,7},{5,4},{6,5},{7,6},{8,11},{9,8},{10,9... | collective-permute-start | bytes 1769480 | tf_op jit(solution)/shard_map/ppermute | solution.py:386
  17.6 1.9 %ends.1 = bf16[2,240,384]{2,1,0:T(8,128)(2,1)} custom-call(bf16[4,192,384]{2,1,0:T(8,128)(2,1)} %bitcast.13, bf16[4,24,384]{2,1,0:T(8,128)(2,1)} %copy-done.13, bf16[4,24,384]{2,1,0:T(8,128)(2,1)} %copy-done.14), custom_call_target="tpu_custom_call" | custom-call | tf_op jit(solution)/shard_map/ends/pallas_call | solution.py:407
  19.5 1.9 %collective-permute-start.2 = (bf16[2,240,384]{2,1,0:T(8,128)(2,1)}, bf16[2,240,384]{2,1,0:T(8,128)(2,1)S(1)}, u32[]{:S(2)}, u32[]{:S(2)}) collective-permute-start(bf16[2,240,384]{2,1,0:T(8,128)(2,1)} %ends.1), channel_id=1, source_target_pairs={{0,4},{4,8},{8,12},{12,16},{16,20},{20,24},{24,28},{28,32},{32,36}... | collective-permute-start | bytes 1105928 | tf_op jit(solution)/shard_map/ppermute | solution.py:408
  21.4 7.1 %collective-permute-done.2.ends_ref = bf16[2,240,384]{2,1,0:T(8,128)(2,1)S(1)} collective-permute-done((bf16[2,240,384]{2,1,0:T(8,128)(2,1)}, bf16[2,240,384]{2,1,0:T(8,128)(2,1)S(1)}, u32[]{:S(2)}, u32[]{:S(2)}) %collective-permute-start.2) | collective-permute-done | bytes 368672 | tf_op jit(solution)/shard_map/ppermute | solution.py:408
  29.3 14.5 %forward.1 = (f32[768,32]{1,0:T(8,128)}, bf16[128,768]{1,0:T(8,128)(2,1)}, bf16[128,768]{1,0:T(8,128)(2,1)}, bf16[128,768]{1,0:T(8,128)(2,1)}, bf16[128,768]{1,0:T(8,128)(2,1)}) custom-call(s32[21]{0:T(128)} %len_ref.3, bf16[4,192,384]{2,1,0:T(8,128)(2,1)} %bitcast.14, bf16[2,240,384]{2,1,0:T(8,128)(2,1)} %copy-done.12, bf16[4,24,384]{2,1,0:T(8,128)(2,1)} %copy-done.13, ...), custom_call_target="tpu_custom_call" | custom-call | tf_op jit(solution)/shard_map/forward/pallas_call | solution.py:415
  43.9 1.7 %collective-permute-start.7 = (bf16[128,768]{1,0:T(8,128)(2,1)}, bf16[128,768]{1,0:T(8,128)(2,1)S(1)}, u32[]{:S(2)}, u32[]{:S(2)}) collective-permute-start(bf16[128,768]{1,0:T(8,128)(2,1)} %get-tuple-element.59), channel_id=1, source_target_pairs={{0,2},{1,3},{2,0},{3,1},{4,6},{5,7},{6,4},{7,5},{8,10},{9,11},{10,... | collective-permute-start | bytes 589832 | tf_op jit(solution)/shard_map/ppermute | solution.py:386
  45.6 1.7 %collective-permute-start.8 = (bf16[128,768]{1,0:T(8,128)(2,1)}, bf16[128,768]{1,0:T(8,128)(2,1)S(1)}, u32[]{:S(2)}, u32[]{:S(2)}) collective-permute-start(bf16[128,768]{1,0:T(8,128)(2,1)} %get-tuple-element.60), channel_id=1, source_target_pairs={{0,3},{1,0},{2,1},{3,2},{4,7},{5,4},{6,5},{7,6},{8,11},{9,8},{10,9... | collective-permute-start | bytes 589832 | tf_op jit(solution)/shard_map/ppermute | solution.py:386
  47.4 5.6 %choose.1 = (bf16[4,768,256]{2,1,0:T(8,128)(2,1)}, bf16[4,768,256]{2,1,0:T(8,128)(2,1)}) custom-call(bf16[4,192,384]{2,1,0:T(8,128)(2,1)} %bitcast.15, bf16[4,192,384]{2,1,0:T(8,128)(2,1)} %copy-done.9, bf16[4,192,384]{2,1,0:T(8,128)(2,1)} %copy-done.10, bf16[4,192,384]{2,1,0:T(8,128)(2,1)} %copy-done.11, bf16[2,384,512]{2,1,0:T(8,128)(2,1)} %constant.2.clone.table_ref), custom_call_target="tpu_custom_call" | custom-call | tf_op jit(solution)/shard_map/choose/pallas_call | solution.py:437
  53.0 3.0 %collective-permute-done.6.a1.refs_1_ = bf16[128,768]{1,0:T(8,128)(2,1)S(1)} collective-permute-done((bf16[128,768]{1,0:T(8,128)(2,1)}, bf16[128,768]{1,0:T(8,128)(2,1)S(1)}, u32[]{:S(2)}, u32[]{:S(2)}) %collective-permute-start.6) | collective-permute-done | bytes 196640 | tf_op jit(solution)/shard_map/ppermute | solution.py:386
  57.3 1.8 %tail.1 = bf16[4,96,384]{2,1,0:T(8,128)(2,1)} custom-call(bf16[128,768]{1,0:T(8,128)(2,1)} %get-tuple-element.66.a0.refs_0_, bf16[128,768]{1,0:T(8,128)(2,1)} %copy-done.1, bf16[128,768]{1,0:T(8,128)(2,1)} %copy-done.2, bf16[128,768]{1,0:T(8,128)(2,1)} %copy-done.3), custom_call_target="tpu_custom_call" | custom-call | tf_op jit(solution)/shard_map/tail/pallas_call | solution.py:451
  59.1 1.9 %collective-permute-start.9 = (bf16[4,96,384]{2,1,0:T(8,128)(2,1)}, bf16[4,96,384]{2,1,0:T(8,128)(2,1)S(1)}, u32[]{:S(2)}, u32[]{:S(2)}) collective-permute-start(bf16[4,96,384]{2,1,0:T(8,128)(2,1)} %tail.1), channel_id=1, source_target_pairs={{8,0},{16,8},{24,16},{32,24},{40,32},{48,40},{56,48},{64,56},{72,6... | collective-permute-start | bytes 884744 | tf_op jit(solution)/shard_map/ppermute | solution.py:459
  63.3 4.6 %collective-permute-done.9.next_ref = bf16[4,96,384]{2,1,0:T(8,128)(2,1)S(1)} collective-permute-done((bf16[4,96,384]{2,1,0:T(8,128)(2,1)}, bf16[4,96,384]{2,1,0:T(8,128)(2,1)S(1)}, u32[]{:S(2)}, u32[]{:S(2)}) %collective-permute-start.9) | collective-permute-done | bytes 294944 | tf_op jit(solution)/shard_map/ppermute | solution.py:459
  70.6 3.0 %collective-permute-start.14 = (f32[8,128]{1,0:T(8,128)}, f32[8,128]{1,0:T(8,128)S(1)}, u32[]{:S(2)}, u32[]{:S(2)}) collective-permute-start(f32[8,128]{1,0:T(8,128)} %clip.1.mid_ref), channel_id=1, source_target_pairs={{0,8},{4,12},{8,16},{12,20},{16,24},{20,28},{24,32},{28,36},{32,40... | collective-permute-start | bytes 12296 | tf_op jit(solution)/shard_map/ppermute | solution.py:383
  73.6 1.5 %collective-permute-done.14 = f32[8,128]{1,0:T(8,128)S(1)} collective-permute-done((f32[8,128]{1,0:T(8,128)}, f32[8,128]{1,0:T(8,128)S(1)}, u32[]{:S(2)}, u32[]{:S(2)}) %collective-permute-start.14) | collective-permute-done | bytes 4128 | tf_op jit(solution)/shard_map/ppermute | solution.py:383
  75.1 3.5 %collective-permute-done.15 = f32[8,128]{1,0:T(8,128)S(1)} collective-permute-done((f32[8,128]{1,0:T(8,128)}, f32[8,128]{1,0:T(8,128)S(1)}, u32[]{:S(2)}, u32[]{:S(2)}) %collective-permute-start.15) | collective-permute-done | bytes 4128 | tf_op jit(solution)/shard_map/ppermute | solution.py:383
  79.3 2.6 %collective-permute-start.16 = (f32[3,8,128]{2,1,0:T(8,128)S(1)}, f32[3,8,128]{2,1,0:T(8,128)S(1)}, u32[]{:S(2)}, u32[]{:S(2)}) collective-permute-start(f32[3,8,128]{2,1,0:T(8,128)S(1)} %pad_maximum_fusion), channel_id=1, source_target_pairs={{0,16},{4,20},{8,24},{12,28},{16,32},{20,36},{24,40},{28,44},{32,4... | collective-permute-start | bytes 36872 | tf_op jit(solution)/shard_map/ppermute | solution.py:383
  82.0 3.6 %collective-permute-start.17 = (f32[3,8,128]{2,1,0:T(8,128)S(1)}, f32[3,8,128]{2,1,0:T(8,128)S(1)}, u32[]{:S(2)}, u32[]{:S(2)}) collective-permute-start(f32[3,8,128]{2,1,0:T(8,128)S(1)} %pad_maximum_fusion), channel_id=1, source_target_pairs={{0,240},{4,244},{8,248},{12,252},{16,0},{20,4},{24,8},{28,12},{32,... | collective-permute-start | bytes 36872 | tf_op jit(solution)/shard_map/ppermute | solution.py:383
  85.6 1.7 %collective-permute-done.16.left_ref = f32[3,8,128]{2,1,0:T(8,128)S(1)} collective-permute-done((f32[3,8,128]{2,1,0:T(8,128)S(1)}, f32[3,8,128]{2,1,0:T(8,128)S(1)}, u32[]{:S(2)}, u32[]{:S(2)}) %collective-permute-start.16) | collective-permute-done | bytes 12320 | tf_op jit(solution)/shard_map/ppermute | solution.py:383
  88.5 15.7 %weight.1 = (f32[3,48,896]{2,1,0:T(8,128)}, bf16[3,48,896]{2,1,0:T(8,128)(2,1)}, bf16[3,48,896]{2,1,0:T(8,128)(2,1)}, bf16[3,48,896]{2,1,0:T(8,128)(2,1)}) custom-call(s32[21]{0:T(128)} %len_ref.3, f32[3,8,128]{2,1,0:T(8,128)} %copy-done.24, f32[8,128]{1,0:T(8,128)} %clip.1.mid_ref, f32[3,8,128]{2,1,0:T(8,128)} %copy-done.25, ...), custom_call_target="tpu_custom_call" | custom-call | tf_op jit(solution)/shard_map/weight/pallas_call | solution.py:477
  105.5 2.9 %collective-permute-start.21 = (bf16[3,48,896]{2,1,0:T(8,128)(2,1)}, bf16[3,48,896]{2,1,0:T(8,128)(2,1)S(1)}, u32[]{:S(2)}, u32[]{:S(2)}) collective-permute-start(bf16[3,48,896]{2,1,0:T(8,128)(2,1)} %get-tuple-element.79), channel_id=1, source_target_pairs={{0,128},{4,132},{8,136},{12,140},{16,144},{20,148},{24,152},{28,15... | collective-permute-start | bytes 774152 | tf_op jit(solution)/shard_map/ppermute | solution.py:389
  109.7 2.6 %collective-permute-done.20.refs_1_ = bf16[3,48,896]{2,1,0:T(8,128)(2,1)S(1)} collective-permute-done((bf16[3,48,896]{2,1,0:T(8,128)(2,1)}, bf16[3,48,896]{2,1,0:T(8,128)(2,1)S(1)}, u32[]{:S(2)}, u32[]{:S(2)}) %collective-permute-start.20) | collective-permute-done | bytes 258080 | tf_op jit(solution)/shard_map/ppermute | solution.py:389
  112.3 3.3 %collective-permute-done.21.refs_2_ = bf16[3,48,896]{2,1,0:T(8,128)(2,1)S(1)} collective-permute-done((bf16[3,48,896]{2,1,0:T(8,128)(2,1)}, bf16[3,48,896]{2,1,0:T(8,128)(2,1)S(1)}, u32[]{:S(2)}, u32[]{:S(2)}) %collective-permute-start.21) | collective-permute-done | bytes 258080 | tf_op jit(solution)/shard_map/ppermute | solution.py:389
  116.7 2.5 %add.1 = (f32[4,24,896]{2,1,0:T(8,128)}, bf16[4,24,896]{2,1,0:T(8,128)(2,1)}) custom-call(f32[3,48,896]{2,1,0:T(8,128)} %get-tuple-element.77.refs_0_, bf16[3,48,896]{2,1,0:T(8,128)(2,1)} %copy-done.17, bf16[3,48,896]{2,1,0:T(8,128)(2,1)} %copy-done.18, bf16[3,48,896]{2,1,0:T(8,128)(2,1)} %copy-done.19), custom_call_target="tpu_custom_call" | custom-call | tf_op jit(solution)/shard_map/add/pallas_call | solution.py:497
  119.7 5.9 %collective-permute-done.23.got_ref = bf16[4,24,896]{2,1,0:T(8,128)(2,1)S(1)} collective-permute-done((bf16[4,24,896]{2,1,0:T(8,128)(2,1)}, bf16[4,24,896]{2,1,0:T(8,128)(2,1)S(1)}, u32[]{:S(2)}, u32[]{:S(2)}) %collective-permute-start.23) | collective-permute-done | bytes 172064 | tf_op jit(solution)/shard_map/ppermute | solution.py:503
  126.4 1.7 %pair.1 = (f32[24,896]{1,0:T(8,128)}, bf16[24,896]{1,0:T(8,128)(2,1)}, bf16[24,896]{1,0:T(8,128)(2,1)}, bf16[24,896]{1,0:T(8,128)(2,1)}) custom-call(f32[4,24,896]{2,1,0:T(8,128)} %get-tuple-element.81.keep_ref, bf16[4,24,896]{2,1,0:T(8,128)(2,1)} %copy-done.20), custom_call_target="tpu_custom_call" | custom-call | tf_op jit(solution)/shard_map/pair/pallas_call | solution.py:504
  128.9 6.1 %collective-permute-start.25 = (bf16[24,896]{1,0:T(8,128)(2,1)}, bf16[24,896]{1,0:T(8,128)(2,1)S(1)}, u32[]{:S(2)}, u32[]{:S(2)}) collective-permute-start(bf16[24,896]{1,0:T(8,128)(2,1)} %get-tuple-element.85), channel_id=1, source_target_pairs={{0,32},{4,36},{8,40},{12,44},{16,48},{20,52},{24,56},{28,60},{32,0... | collective-permute-start | bytes 129032 | tf_op jit(solution)/shard_map/ppermute | solution.py:392
  135.0 2.7 %collective-permute-done.25.refs_2_ = bf16[24,896]{1,0:T(8,128)(2,1)S(1)} collective-permute-done((bf16[24,896]{1,0:T(8,128)(2,1)}, bf16[24,896]{1,0:T(8,128)(2,1)S(1)}, u32[]{:S(2)}, u32[]{:S(2)}) %collective-permute-start.25) | collective-permute-done | bytes 43040 | tf_op jit(solution)/shard_map/ppermute | solution.py:392
  137.7 2.4 %collective-permute-done.26.refs_3_ = bf16[24,896]{1,0:T(8,128)(2,1)S(1)} collective-permute-done((bf16[24,896]{1,0:T(8,128)(2,1)}, bf16[24,896]{1,0:T(8,128)(2,1)S(1)}, u32[]{:S(2)}, u32[]{:S(2)}) %collective-permute-start.26) | collective-permute-done | bytes 43040 | tf_op jit(solution)/shard_map/ppermute | solution.py:392
  140.8 1.8 %last.1 = (f32[6,27,96]{2,1,0:T(8,128)}, f32[6,8]{1,0:T(8,128)}, f32[1,1]{1,0:T(1,128)}) custom-call(f32[24,896]{1,0:T(8,128)} %get-tuple-element.83.refs_0_, bf16[24,896]{1,0:T(8,128)(2,1)} %copy-done.21, bf16[24,896]{1,0:T(8,128)(2,1)} %copy-done.22, bf16[24,896]{1,0:T(8,128)(2,1)} %copy-done.23), custom_call_target="tpu_custom_call" | custom-call | tf_op jit(solution)/shard_map/last/pallas_call | solution.py:511
  (85 shorter events, 20.3 us)
Async XLA Ops:
  2.4 5.7 %collective-permute-start = (bf16[4,24,384]{2,1,0:T(8,128)(2,1)}, bf16[4,24,384]{2,1,0:T(8,128)(2,1)S(1)}, u32[]{:S(2)}, u32[]{:S(2)}) collective-permute-start(bf16[4,24,384]{2,1,0:T(8,128)(2,1)} %get-tuple-element.47), channel_id=1, source_target_pairs={{0,1},{1,2},{2,3},{4,5},{5,6},{6,7},{8,9},{9,10},{10,11},{12,13},{... | collective-permute-start | bytes 221192 | tf_op jit(solution)/shard_map/ppermute | solution.py:402
  5.8 6.5 %collective-permute-start.1 = (bf16[4,24,384]{2,1,0:T(8,128)(2,1)}, bf16[4,24,384]{2,1,0:T(8,128)(2,1)S(1)}, u32[]{:S(2)}, u32[]{:S(2)}) collective-permute-start(bf16[4,24,384]{2,1,0:T(8,128)(2,1)} %get-tuple-element.48), channel_id=1, source_target_pairs={{1,0},{2,1},{3,2},{5,4},{6,5},{7,6},{9,8},{10,9},{11,10},{13,12},{... | collective-permute-start | bytes 221192 | tf_op jit(solution)/shard_map/ppermute | solution.py:403
  8.0 9.5 %copy-start.13 = (bf16[4,24,384]{2,1,0:T(8,128)(2,1)}, bf16[4,24,384]{2,1,0:T(8,128)(2,1)S(1)}, u32[]{:S(2)}) copy-start(bf16[4,24,384]{2,1,0:T(8,128)(2,1)S(1)} %collective-permute-done.top_ref) | copy-start | bytes 221188
  12.2 31.6 %collective-permute-start.3 = (bf16[4,192,384]{2,1,0:T(8,128)(2,1)}, bf16[4,192,384]{2,1,0:T(8,128)(2,1)S(1)}, u32[]{:S(2)}, u32[]{:S(2)}) collective-permute-start(bf16[4,192,384]{2,1,0:T(8,128)(2,1)} %bitcast.10), channel_id=1, source_target_pairs={{0,1},{1,2},{2,3},{3,0},{4,5},{5,6},{6,7},{7,4},{8,9},{9,10},{10,1... | collective-permute-start | bytes 1769480 | tf_op jit(solution)/shard_map/ppermute | solution.py:386
  13.7 30.1 %collective-permute-start.4 = (bf16[4,192,384]{2,1,0:T(8,128)(2,1)}, bf16[4,192,384]{2,1,0:T(8,128)(2,1)S(1)}, u32[]{:S(2)}, u32[]{:S(2)}) collective-permute-start(bf16[4,192,384]{2,1,0:T(8,128)(2,1)} %bitcast.11), channel_id=1, source_target_pairs={{0,2},{1,3},{2,0},{3,1},{4,6},{5,7},{6,4},{7,5},{8,10},{9,11},{10,... | collective-permute-start | bytes 1769480 | tf_op jit(solution)/shard_map/ppermute | solution.py:386
  15.0 28.9 %collective-permute-start.5 = (bf16[4,192,384]{2,1,0:T(8,128)(2,1)}, bf16[4,192,384]{2,1,0:T(8,128)(2,1)S(1)}, u32[]{:S(2)}, u32[]{:S(2)}) collective-permute-start(bf16[4,192,384]{2,1,0:T(8,128)(2,1)} %bitcast.12), channel_id=1, source_target_pairs={{0,3},{1,0},{2,1},{3,2},{4,7},{5,4},{6,5},{7,6},{8,11},{9,8},{10,9... | collective-permute-start | bytes 1769480 | tf_op jit(solution)/shard_map/ppermute | solution.py:386
  19.5 9.0 %collective-permute-start.2 = (bf16[2,240,384]{2,1,0:T(8,128)(2,1)}, bf16[2,240,384]{2,1,0:T(8,128)(2,1)S(1)}, u32[]{:S(2)}, u32[]{:S(2)}) collective-permute-start(bf16[2,240,384]{2,1,0:T(8,128)(2,1)} %ends.1), channel_id=1, source_target_pairs={{0,4},{4,8},{8,12},{12,16},{16,20},{20,24},{24,28},{28,32},{32,36}... | collective-permute-start | bytes 1105928 | tf_op jit(solution)/shard_map/ppermute | solution.py:408
  43.8 12.8 %copy-start = (bf16[128,768]{1,0:T(8,128)(2,1)S(1)}, bf16[128,768]{1,0:T(8,128)(2,1)}, u32[]{:S(2)}) copy-start(bf16[128,768]{1,0:T(8,128)(2,1)} %get-tuple-element.66.a0.refs_0_) | copy-start | bytes 589828
  43.8 12.2 %collective-permute-start.6 = (bf16[128,768]{1,0:T(8,128)(2,1)}, bf16[128,768]{1,0:T(8,128)(2,1)S(1)}, u32[]{:S(2)}, u32[]{:S(2)}) collective-permute-start(bf16[128,768]{1,0:T(8,128)(2,1)} %get-tuple-element.58), channel_id=1, source_target_pairs={{0,1},{1,2},{2,3},{3,0},{4,5},{5,6},{6,7},{7,4},{8,9},{9,10},{10,1... | collective-permute-start | bytes 589832 | tf_op jit(solution)/shard_map/ppermute | solution.py:386
  43.9 12.1 %collective-permute-start.7 = (bf16[128,768]{1,0:T(8,128)(2,1)}, bf16[128,768]{1,0:T(8,128)(2,1)S(1)}, u32[]{:S(2)}, u32[]{:S(2)}) collective-permute-start(bf16[128,768]{1,0:T(8,128)(2,1)} %get-tuple-element.59), channel_id=1, source_target_pairs={{0,2},{1,3},{2,0},{3,1},{4,6},{5,7},{6,4},{7,5},{8,10},{9,11},{10,... | collective-permute-start | bytes 589832 | tf_op jit(solution)/shard_map/ppermute | solution.py:386
  45.6 11.0 %collective-permute-start.8 = (bf16[128,768]{1,0:T(8,128)(2,1)}, bf16[128,768]{1,0:T(8,128)(2,1)S(1)}, u32[]{:S(2)}, u32[]{:S(2)}) collective-permute-start(bf16[128,768]{1,0:T(8,128)(2,1)} %get-tuple-element.60), channel_id=1, source_target_pairs={{0,3},{1,0},{2,1},{3,2},{4,7},{5,4},{6,5},{7,6},{8,11},{9,8},{10,9... | collective-permute-start | bytes 589832 | tf_op jit(solution)/shard_map/ppermute | solution.py:386
  56.6 30.6 %collective-permute-start.19 = (bf16[4,768,256]{2,1,0:T(8,128)(2,1)}, bf16[4,768,256]{2,1,0:T(8,128)(2,1)S(1)}, u32[]{:S(2)}, u32[]{:S(2)}) collective-permute-start(bf16[4,768,256]{2,1,0:T(8,128)(2,1)} %get-tuple-element.76), channel_id=1, source_target_pairs={{0,4},{4,0},{8,12},{12,8},{16,20},{20,16},{24,28},{28,24},{32,36},... | collective-permute-start | bytes 4718600 | tf_op jit(solution)/shard_map/ppermute | solution.py:380
  56.7 4.9 %collective-permute-start.10 = (bf16[128,768]{1,0:T(8,128)(2,1)S(1)}, bf16[128,768]{1,0:T(8,128)(2,1)S(1)}, u32[]{:S(2)}, u32[]{:S(2)}) collective-permute-start(bf16[128,768]{1,0:T(8,128)(2,1)S(1)} %copy-done), channel_id=1, source_target_pairs={{0,4},{4,0},{8,12},{12,8},{16,20},{20,16},{24,28},{28,24},{32,36},... | collective-permute-start | bytes 589832 | tf_op jit(solution)/shard_map/ppermute | solution.py:380
  59.1 8.8 %collective-permute-start.9 = (bf16[4,96,384]{2,1,0:T(8,128)(2,1)}, bf16[4,96,384]{2,1,0:T(8,128)(2,1)S(1)}, u32[]{:S(2)}, u32[]{:S(2)}) collective-permute-start(bf16[4,96,384]{2,1,0:T(8,128)(2,1)} %tail.1), channel_id=1, source_target_pairs={{8,0},{16,8},{24,16},{32,24},{40,32},{48,40},{56,48},{64,56},{72,6... | collective-permute-start | bytes 884744 | tf_op jit(solution)/shard_map/ppermute | solution.py:459
  61.0 1.7 %collective-permute-start.11 = (bf16[128,768]{1,0:T(8,128)(2,1)}, bf16[128,768]{1,0:T(8,128)(2,1)S(1)}, u32[]{:S(2)}, u32[]{:S(2)}) collective-permute-start(bf16[128,768]{1,0:T(8,128)(2,1)} %copy-done.1), channel_id=1, source_target_pairs={{0,4},{4,0},{8,12},{12,8},{16,20},{20,16},{24,28},{28,24},{32,36},... | collective-permute-start | bytes 589832 | tf_op jit(solution)/shard_map/ppermute | solution.py:380
  61.1 1.9 %collective-permute-start.12 = (bf16[128,768]{1,0:T(8,128)(2,1)}, bf16[128,768]{1,0:T(8,128)(2,1)S(1)}, u32[]{:S(2)}, u32[]{:S(2)}) collective-permute-start(bf16[128,768]{1,0:T(8,128)(2,1)} %copy-done.2), channel_id=1, source_target_pairs={{0,4},{4,0},{8,12},{12,8},{16,20},{20,16},{24,28},{28,24},{32,36},... | collective-permute-start | bytes 589832 | tf_op jit(solution)/shard_map/ppermute | solution.py:380
  61.6 7.6 %copy-start.5 = (bf16[128,768]{1,0:T(8,128)(2,1)}, bf16[128,768]{1,0:T(8,128)(2,1)S(1)}, u32[]{:S(2)}) copy-start(bf16[128,768]{1,0:T(8,128)(2,1)S(1)} %collective-permute-done.10.refs_4_.b0) | copy-start | bytes 589828
  61.6 1.7 %collective-permute-start.13 = (bf16[128,768]{1,0:T(8,128)(2,1)}, bf16[128,768]{1,0:T(8,128)(2,1)S(1)}, u32[]{:S(2)}, u32[]{:S(2)}) collective-permute-start(bf16[128,768]{1,0:T(8,128)(2,1)} %copy-done.3), channel_id=1, source_target_pairs={{0,4},{4,0},{8,12},{12,8},{16,20},{20,16},{24,28},{28,24},{32,36},... | collective-permute-start | bytes 589832 | tf_op jit(solution)/shard_map/ppermute | solution.py:380
  62.7 6.5 %copy-start.6 = (bf16[128,768]{1,0:T(8,128)(2,1)}, bf16[128,768]{1,0:T(8,128)(2,1)S(1)}, u32[]{:S(2)}) copy-start(bf16[128,768]{1,0:T(8,128)(2,1)S(1)} %collective-permute-done.11.refs_5_.b1) | copy-start | bytes 589828
  67.9 19.4 %copy-start.15 = (bf16[4,96,384]{2,1,0:T(8,128)(2,1)}, bf16[4,96,384]{2,1,0:T(8,128)(2,1)S(1)}, u32[]{:S(2)}) copy-start(bf16[4,96,384]{2,1,0:T(8,128)(2,1)S(1)} %collective-permute-done.9.next_ref) | copy-start | bytes 884740
  67.9 19.4 %collective-permute-start.18 = (bf16[4,96,384]{2,1,0:T(8,128)(2,1)S(1)}, bf16[4,96,384]{2,1,0:T(8,128)(2,1)S(1)}, u32[]{:S(2)}, u32[]{:S(2)}) collective-permute-start(bf16[4,96,384]{2,1,0:T(8,128)(2,1)S(1)} %collective-permute-done.9.next_ref), channel_id=1, source_target_pairs={{0,4},{8,12},{16,20},{24,28},{32,36},{40,44},{48,52},{56,60},{64,6... | collective-permute-start | bytes 884744 | tf_op jit(solution)/shard_map/ppermute | solution.py:461
  70.6 4.6 %collective-permute-start.14 = (f32[8,128]{1,0:T(8,128)}, f32[8,128]{1,0:T(8,128)S(1)}, u32[]{:S(2)}, u32[]{:S(2)}) collective-permute-start(f32[8,128]{1,0:T(8,128)} %clip.1.mid_ref), channel_id=1, source_target_pairs={{0,8},{4,12},{8,16},{12,20},{16,24},{20,28},{24,32},{28,36},{32,40... | collective-permute-start | bytes 12296 | tf_op jit(solution)/shard_map/ppermute | solution.py:383
  73.6 5.1 %collective-permute-start.15 = (f32[8,128]{1,0:T(8,128)}, f32[8,128]{1,0:T(8,128)S(1)}, u32[]{:S(2)}, u32[]{:S(2)}) collective-permute-start(f32[8,128]{1,0:T(8,128)} %clip.1.mid_ref), channel_id=1, source_target_pairs={{0,248},{4,252},{8,0},{12,4},{16,8},{20,12},{24,16},{28,20},{32,24... | collective-permute-start | bytes 12296 | tf_op jit(solution)/shard_map/ppermute | solution.py:383
  79.3 7.9 %collective-permute-start.16 = (f32[3,8,128]{2,1,0:T(8,128)S(1)}, f32[3,8,128]{2,1,0:T(8,128)S(1)}, u32[]{:S(2)}, u32[]{:S(2)}) collective-permute-start(f32[3,8,128]{2,1,0:T(8,128)S(1)} %pad_maximum_fusion), channel_id=1, source_target_pairs={{0,16},{4,20},{8,24},{12,28},{16,32},{20,36},{24,40},{28,44},{32,4... | collective-permute-start | bytes 36872 | tf_op jit(solution)/shard_map/ppermute | solution.py:383
  82.0 5.3 %collective-permute-start.17 = (f32[3,8,128]{2,1,0:T(8,128)S(1)}, f32[3,8,128]{2,1,0:T(8,128)S(1)}, u32[]{:S(2)}, u32[]{:S(2)}) collective-permute-start(f32[3,8,128]{2,1,0:T(8,128)S(1)} %pad_maximum_fusion), channel_id=1, source_target_pairs={{0,240},{4,244},{8,248},{12,252},{16,0},{20,4},{24,8},{28,12},{32,... | collective-permute-start | bytes 36872 | tf_op jit(solution)/shard_map/ppermute | solution.py:383
  104.2 8.1 %collective-permute-start.20 = (bf16[3,48,896]{2,1,0:T(8,128)(2,1)}, bf16[3,48,896]{2,1,0:T(8,128)(2,1)S(1)}, u32[]{:S(2)}, u32[]{:S(2)}) collective-permute-start(bf16[3,48,896]{2,1,0:T(8,128)(2,1)} %get-tuple-element.78), channel_id=1, source_target_pairs={{0,64},{4,68},{8,72},{12,76},{16,80},{20,84},{24,88},{28,92},{32,9... | collective-permute-start | bytes 774152 | tf_op jit(solution)/shard_map/ppermute | solution.py:389
  105.5 10.2 %collective-permute-start.21 = (bf16[3,48,896]{2,1,0:T(8,128)(2,1)}, bf16[3,48,896]{2,1,0:T(8,128)(2,1)S(1)}, u32[]{:S(2)}, u32[]{:S(2)}) collective-permute-start(bf16[3,48,896]{2,1,0:T(8,128)(2,1)} %get-tuple-element.79), channel_id=1, source_target_pairs={{0,128},{4,132},{8,136},{12,140},{16,144},{20,148},{24,152},{28,15... | collective-permute-start | bytes 774152 | tf_op jit(solution)/shard_map/ppermute | solution.py:389
  108.4 7.6 %collective-permute-start.22 = (bf16[3,48,896]{2,1,0:T(8,128)(2,1)}, bf16[3,48,896]{2,1,0:T(8,128)(2,1)S(1)}, u32[]{:S(2)}, u32[]{:S(2)}) collective-permute-start(bf16[3,48,896]{2,1,0:T(8,128)(2,1)} %get-tuple-element.80), channel_id=1, source_target_pairs={{0,192},{4,196},{8,200},{12,204},{16,208},{20,212},{24,216},{28,22... | collective-permute-start | bytes 774152 | tf_op jit(solution)/shard_map/ppermute | solution.py:389
  119.1 6.5 %collective-permute-start.23 = (bf16[4,24,896]{2,1,0:T(8,128)(2,1)}, bf16[4,24,896]{2,1,0:T(8,128)(2,1)S(1)}, u32[]{:S(2)}, u32[]{:S(2)}) collective-permute-start(bf16[4,24,896]{2,1,0:T(8,128)(2,1)} %get-tuple-element.82), channel_id=1, source_target_pairs={{0,8},{4,12},{8,0},{12,4},{16,24},{20,28},{24,16},{28,20},{32,40},... | collective-permute-start | bytes 516104 | tf_op jit(solution)/shard_map/ppermute | solution.py:503
  128.1 6.9 %collective-permute-start.24 = (bf16[24,896]{1,0:T(8,128)(2,1)}, bf16[24,896]{1,0:T(8,128)(2,1)S(1)}, u32[]{:S(2)}, u32[]{:S(2)}) collective-permute-start(bf16[24,896]{1,0:T(8,128)(2,1)} %get-tuple-element.84), channel_id=1, source_target_pairs={{0,16},{4,20},{8,24},{12,28},{16,32},{20,36},{24,40},{28,44},{32,4... | collective-permute-start | bytes 129032 | tf_op jit(solution)/shard_map/ppermute | solution.py:392
  128.9 8.8 %collective-permute-start.25 = (bf16[24,896]{1,0:T(8,128)(2,1)}, bf16[24,896]{1,0:T(8,128)(2,1)S(1)}, u32[]{:S(2)}, u32[]{:S(2)}) collective-permute-start(bf16[24,896]{1,0:T(8,128)(2,1)} %get-tuple-element.85), channel_id=1, source_target_pairs={{0,32},{4,36},{8,40},{12,44},{16,48},{20,52},{24,56},{28,60},{32,0... | collective-permute-start | bytes 129032 | tf_op jit(solution)/shard_map/ppermute | solution.py:392
  135.0 5.1 %collective-permute-start.26 = (bf16[24,896]{1,0:T(8,128)(2,1)}, bf16[24,896]{1,0:T(8,128)(2,1)S(1)}, u32[]{:S(2)}, u32[]{:S(2)}) collective-permute-start(bf16[24,896]{1,0:T(8,128)(2,1)} %get-tuple-element.86), channel_id=1, source_target_pairs={{0,48},{4,52},{8,56},{12,60},{16,0},{20,4},{24,8},{28,12},{32,16},... | collective-permute-start | bytes 129032 | tf_op jit(solution)/shard_map/ppermute | solution.py:392
  (21 other events, 48.9 us)
